TPU v7x, 512 devices: a whole 4x4x16 slice. The times are simulated.
512 devices in a mesh: dp: 64 (over z, y_lo, core), tensor: 8 (over x, y_hi).
Axes of the slice: x: 4, y: 4 (y_hi: 2, y_lo: 2; y = y_hi * 2 + y_lo), z: 16, core: 2. Of those that a mesh axis runs over, the one named last changes fastest.
Arguments:
- activations: bfloat16 [98304, 2048], P('dp', 'tensor'), may hold values from -6 to 6
- out_grads: bfloat16 [98304, 2048], P('dp', 'tensor'), may hold values from -0.001953125 to 0.001953125
- left_stat: float32 [2048, 2048], P('dp', 'tensor'), may hold values from -1 to 11, as said below
- right_stat: float32 [2048, 2048], P('dp', 'tensor'), may hold values from -1 to 11, as said below
Outputs:
- left_new: float32 [2048, 2048], P('dp', 'tensor')
- right_new: float32 [2048, 2048], P('dp', 'tensor')
- update: float32 [2048, 2048], P('dp', 'tensor')
Inputs may be any that keep to these rules, and one draw needn't show every extreme that they name: `left_stat`: symmetric, with a positive diagonal. `right_stat`: symmetric, with a positive diagonal.
All inputs are finite; a program needn't handle non-finite values.
Results may differ from a plain program's by a relative error of at most 0.0012.
Values may be sent and summed in bfloat16 or wider, within the bound.
A program may use at most 64 MiB of HBM per device.

v0:
```python
import jax
import jax.numpy as jnp
from jax import lax
from jax.sharding import Mesh
from jax.sharding import PartitionSpec as P

TENSOR = ("tensor_0", "tensor_1")
DP = ("dp_0", "dp_1", "dp_2")
DP_TENSOR = ("dp_0", "dp_1", "dp_2", "tensor_0", "tensor_1")


def in_blocks(x, dim, length):
    lengths = x.shape
    blocks = x.reshape(*lengths[:dim], length, lengths[dim] // length, *lengths[dim + 1 :])
    return jnp.moveaxis(blocks, dim, 0)


def sum_at_owner(x, axis, dim):
    length = lax.axis_size(axis)
    blocks = lax.all_to_all(in_blocks(x, dim, length), axis, 0, 0, tiled=True)
    return jnp.sum(blocks, axis=0)


def in_order(blocks, dim):
    blocks = jnp.moveaxis(blocks, 0, dim)
    lengths = blocks.shape
    return blocks.reshape(*lengths[:dim], lengths[dim] * lengths[dim + 1], *lengths[dim + 2 :])


def gather_in_order(x, axes, turns):
    blocks = x
    for k in turns:
        blocks = lax.all_gather(blocks, axes[k])
    done = turns[::-1]
    back = [done.index(k) for k in range(len(axes))]
    blocks = blocks.transpose(*back, *range(len(axes), blocks.ndim))
    return blocks.reshape(-1, *x.shape)


def gathered_by_axis(x, axes, turns, dim):
    return in_order(gather_in_order(x, axes, turns), dim)


def side_by_side(arrays, axis, dim, along):
    both = jnp.concatenate(arrays, axis=along)
    result, at, gathered = (sum_at_owner(both, axis, dim), 0, [])
    for a in arrays:
        gathered.append(lax.slice_in_dim(result, at, at + a.shape[along], axis=along))
        at += a.shape[along]
    return tuple(gathered)


def by_axis(x, axes):
    for axis in axes:
        x = lax.psum(x, axis)
    return x


def sent_to_all(x, axis):
    length = lax.axis_size(axis)
    return lax.all_to_all(jnp.broadcast_to(x[None], (length, *x.shape)), axis, 0, 0, tiled=True)


def gather_directly(x, axis, dim):
    return in_order(sent_to_all(x, axis), dim)


def local(activations, out_grads, left_stat, right_stat):
    highest = lax.Precision.HIGHEST
    tensor_count = lax.axis_size(TENSOR)
    dp_count = lax.axis_size(DP)
    col_count = out_grads.shape[1]
    full_order = col_count * tensor_count
    row_count = full_order // dp_count
    grad_terms = lax.dot_general(
        lax.all_gather(activations, TENSOR, axis=1, tiled=True),
        out_grads,
        (((0,), (0,)), ((), ())),
        preferred_element_type=jnp.float32,
    )
    grad_block = sum_at_owner(grad_terms, DP, 0)
    grad_cols = gathered_by_axis(grad_block, DP, (1, 0, 2), 0)
    left_part = lax.dot_general(
        grad_block,
        grad_cols,
        (((1,), (1,)), ((), ())),
        precision=highest,
        preferred_element_type=jnp.float32,
    )
    dp_place = lax.axis_index(DP)
    row_start = dp_place * row_count
    tensor_rows = lax.all_to_all(grad_cols, TENSOR, split_axis=0, concat_axis=1, tiled=True)
    strip_cols = lax.dynamic_slice_in_dim(tensor_rows, row_start, row_count, 1)
    right_part = lax.dot_general(
        strip_cols,
        tensor_rows,
        (((0,), (0,)), ((), ())),
        precision=highest,
        preferred_element_type=jnp.float32,
    )
    left_sum, right_sum = side_by_side((left_part, right_part), TENSOR, 1, 0)
    left_new = 0.9 * left_stat + 0.1 * left_sum
    right_new = 0.9 * right_stat + 0.1 * right_sum
    left_sq = jnp.sum(left_new * left_new)
    right_sq = jnp.sum(right_new * right_new)
    grad_sq = jnp.sum(grad_block * grad_block)
    left_total, right_total, grad_total = (
        by_axis(left_sq, DP_TENSOR),
        by_axis(right_sq, DP_TENSOR),
        by_axis(grad_sq, DP_TENSOR),
    )
    left_scale = jnp.sqrt(left_total / full_order + 1e-06)
    right_scale = jnp.sqrt(right_total / full_order + 1e-06)
    left_whole = gather_directly(left_new, TENSOR, 1)
    left_product = jnp.dot(
        left_whole, grad_cols, precision=highest, preferred_element_type=jnp.float32
    )
    pre_left = 5.0 * grad_block - left_product / left_scale
    pre_rows = gather_directly(pre_left, TENSOR, 1)
    right_product = jnp.dot(
        pre_rows,
        lax.all_gather(right_new.astype(jnp.bfloat16), DP, axis=0, tiled=True).astype(jnp.float32),
        precision=highest,
        preferred_element_type=jnp.float32,
    )
    pre_block = 5.0 * pre_left - right_product / right_scale
    pre_sq = jnp.sum(pre_block * pre_block)
    pre_total = by_axis(pre_sq, DP_TENSOR)
    factor = jnp.sqrt(grad_total + 1e-06) / jnp.sqrt(pre_total + 1e-06)
    return (left_new, right_new, pre_block * factor)


def solution(mesh):
    finer = Mesh(
        mesh.devices.reshape(16, 2, 2, 4, 2), ("dp_0", "dp_1", "dp_2", "tensor_0", "tensor_1")
    )
    placed = (P(DP, TENSOR), P(DP, TENSOR), P(DP, TENSOR), P(DP, TENSOR))
    return jax.shard_map(
        local,
        mesh=finer,
        in_specs=placed,
        out_specs=(P(DP, TENSOR), P(DP, TENSOR), P(DP, TENSOR)),
        check_vma=False,
    )
```

profile of v0, /device:TPU:1, one launch (start us, length us, event | category | flops | bytes accessed | tf_op | source)
XLA Modules:
  0.0 580.9 jit_solution(15723450914595324753)
XLA Ops:
  7.2 0.0 copy-start
  7.2 0.0 all-gather.8.cloned.1.call-start
  7.2 0.7 all-gather.8.cloned.1.call-update
  7.9 0.0 all-gather.12.cloned.1.call-start
  8.0 122.3 %all-gather.8.cloned.1.call-done = bf16[1536,2048]{1,0:T(8,128)(2,1)} async-done(((bf16[1536,256]{1,0:T(8,128)(2,1)}), bf16[1536,2048]{1,0:T(8,128)(2,1)}) %all-gather.8.cloned.1.call-update) | async-done | bytes 6291472 | tf_op jit(solution)/shard_map/all_gather | solution.py:76
  130.3 0.0 copy-done
  130.3 4.7 fusion.10
  135.0 112.4 %all_to_all.39 = f32[64,32,256]{2,1,0:T(8,128)S(1)} all-to-all(f32[64,32,256]{2,1,0:T(8,128)S(1)} %bitcast.35), channel_id=1, replica_groups=mesh['dp_0'=16,'dp_1'=2,'dp_2'=2,'tensor_0'=4,'tensor_1'=2] {'dp_0','dp_..., dimensions={0} | all-to-all | bytes 4194304 | tf_op jit(solution)/shard_map/all_to_all | solution.py:20
  247.5 0.1 reduce_sum.54
  247.6 4.8 all-gather
  252.4 0.0 all-gather.12.cloned.1.call-update
  252.4 0.0 all-gather.14.cloned.1.call-start
  252.5 53.7 %all-gather.12.cloned.1.call-done = f32[32,32,256]{2,1,0:T(8,128)} async-done(((f32[2,32,256]{2,1,0:T(8,128)}), f32[32,32,256]{2,1,0:T(8,128)}) %all-gather.12.cloned.1.call-update) | async-done | bytes 1048592 | tf_op jit(solution)/shard_map/all_gather | solution.py:33
  306.1 0.0 all-gather.14.cloned.1.call-update
  306.2 30.9 %all-gather.14.cloned.1.call-done = f32[32,2,32,256]{3,2,1,0:T(8,128)} async-done(((f32[16,2,32,256]{3,2,1,0:T(8,128)}), f32[32,2,32,256]{3,2,1,0:T(8,128)}) %all-gather.14.cloned.1.call-update) | async-done | bytes 2097168 | tf_op jit(solution)/shard_map/all_gather | solution.py:33
  337.1 3.2 copy.11
  340.3 5.4 all-to-all-start.1
  345.7 0.0 all-gather.10.cloned.1.call-start
  345.8 3.6 fusion.11
  349.4 27.4 %all-to-all-done.1 = f32[8,256,256]{2,1,0:T(8,128)S(1)} async-done(((f32[8,256,256]{2,1,0:T(8,128)}), f32[8,256,256]{2,1,0:T(8,128)S(1)}, u32[]{:S(2)}, u32[]{:S(2)}) %all-to-all-start.1) | async-done | bytes 2097184 | tf_op jit(solution)/shard_map/all_to_all | solution.py:92
  376.8 0.0 copy-start.1
  376.8 1.3 copy-done.1
  378.1 1.9 copy.13
  380.0 2.0 fusion.4
  382.0 0.0 copy-start.4
  382.0 0.0 copy-start.5
  382.1 12.7 %all_to_all.40 = f32[8,64,256]{2,1,0:T(8,128)S(1)} all-to-all(f32[8,64,256]{2,1,0:T(8,128)S(1)} %bitcast.37), channel_id=1, replica_groups=mesh['dp_0'=16,'dp_1'=2,'dp_2'=2,'tensor_0'=4,'tensor_1'=2] {'tensor_0',..., dimensions={0} | all-to-all | bytes 1048576 | tf_op jit(solution)/shard_map/all_to_all | solution.py:20
  394.9 0.0 copy-done.4
  394.9 0.0 copy-done.5
  394.9 1.2 fusion.7
  396.1 0.0 copy-start.2
  396.1 0.0 copy-start.3
  396.1 0.0 all-gather.10.cloned.1.call-update
  396.1 0.7 broadcast_in_dim.4
  396.9 3.4 all-to-all-start.3
  400.3 0.7 multiply_reduce_fusion.2
  401.0 25.5 %all-reduce.1 = (f32[]{:T(128)}, f32[]{:T(128)}) all-reduce(f32[]{:T(128)} %get-tuple-element.27, f32[]{:T(128)} %multiply_reduce_fusion.2), channel_id=1, replica_groups=mesh['dp_0'=16,'dp_1'=2,'dp_2'=2,'tensor_0'=4,'tensor_1'=2] {'dp_0'}, use_global_device_ids=true, to_apply=%region_3.0 | all-reduce | flops 2 | bytes 16 | tf_op jit(solution)/shard_map/psum | solution.py:55
  426.4 4.8 all-reduce.9
  431.3 12.8 %all-reduce.7 = (f32[]{:T(128)}, f32[]{:T(128)}) all-reduce(f32[]{:T(128)} %get-tuple-element.21, f32[]{:T(128)} %get-tuple-element.22), channel_id=1, replica_groups=mesh['dp_0'=16,'dp_1'=2,'dp_2'=2,'tensor_0'=4,'tensor_1'=2] {'dp_2'}, use_global_device_ids=true, to_apply=%region_5.0 | all-reduce | flops 2 | bytes 16 | tf_op jit(solution)/shard_map/psum | solution.py:55
  444.0 9.6 %all-reduce.3 = (f32[]{:T(128)}, f32[]{:T(128)}) all-reduce(f32[]{:T(128)} %get-tuple-element.17, f32[]{:T(128)} %get-tuple-element.18), channel_id=1, replica_groups=mesh['dp_0'=16,'dp_1'=2,'dp_2'=2,'tensor_0'=4,'tensor_1'=2] {'tensor_0'}, use_global_device_ids=true, to_apply=%region_6.0 | all-reduce | flops 2 | bytes 16 | tf_op jit(solution)/shard_map/psum | solution.py:55
  453.6 6.0 %all-reduce.5 = (f32[]{:T(128)}, f32[]{:T(128)}) all-reduce(f32[]{:T(128)} %get-tuple-element.9, f32[]{:T(128)} %get-tuple-element.10), channel_id=1, replica_groups=mesh['dp_0'=16,'dp_1'=2,'dp_2'=2,'tensor_0'=4,'tensor_1'=2] {'tensor_1'}, use_global_device_ids=true, to_apply=%region_7.0 | all-reduce | flops 2 | bytes 16 | tf_op jit(solution)/shard_map/psum | solution.py:55
  460.3 0.0 all-to-all-done.3
  460.4 2.7 fusion.1
  463.1 0.7 broadcast_in_dim.5
  463.8 0.0 copy-done.2
  463.8 0.0 copy-done.3
  463.8 4.6 all-to-all-start.4
  468.4 0.6 multiply_reduce_fusion.1
  469.6 6.2 %all-to-all-done.4 = f32[8,32,256]{2,1,0:T(8,128)S(1)} async-done(((f32[8,32,256]{2,1,0:T(8,128)}), f32[8,32,256]{2,1,0:T(8,128)S(1)}, u32[]{:S(2)}, u32[]{:S(2)}) %all-to-all-start.4) | async-done | bytes 262176 | tf_op jit(solution)/shard_map/all_to_all | solution.py:61
  475.8 41.2 %all-gather.10.cloned.1.call-done = bf16[2048,256]{1,0:T(8,128)(2,1)} async-done(((bf16[32,256]{1,0:T(8,128)(2,1)}), bf16[2048,256]{1,0:T(8,128)(2,1)}) %all-gather.10.cloned.1.call-update) | async-done | bytes 1048592 | tf_op jit(solution)/shard_map/all_gather | solution.py:122
  516.9 2.4 multiply_reduce_fusion
  519.4 22.4 %all-reduce = (f32[]{:T(128)}, f32[]{:T(128)}) all-reduce(f32[]{:T(128)} %multiply_reduce_fusion.1, f32[]{:T(128)} %get-tuple-element.29), channel_id=1, replica_groups=mesh['dp_0'=16,'dp_1'=2,'dp_2'=2,'tensor_0'=4,'tensor_1'=2] {'dp_0'}, use_global_device_ids=true, to_apply=%region_15.0 | all-reduce | flops 2 | bytes 16 | tf_op jit(solution)/shard_map/psum | solution.py:55
  541.8 4.5 all-reduce.8
  546.3 11.1 %all-reduce.6 = (f32[]{:T(128)}, f32[]{:T(128)}) all-reduce(f32[]{:T(128)} %get-tuple-element.19, f32[]{:T(128)} %get-tuple-element.20), channel_id=1, replica_groups=mesh['dp_0'=16,'dp_1'=2,'dp_2'=2,'tensor_0'=4,'tensor_1'=2] {'dp_2'}, use_global_device_ids=true, to_apply=%region_17.0 | all-reduce | flops 2 | bytes 16 | tf_op jit(solution)/shard_map/psum | solution.py:55
  557.4 9.2 %all-reduce.2 = (f32[]{:T(128)}, f32[]{:T(128)}) all-reduce(f32[]{:T(128)} %get-tuple-element.15, f32[]{:T(128)} %get-tuple-element.16), channel_id=1, replica_groups=mesh['dp_0'=16,'dp_1'=2,'dp_2'=2,'tensor_0'=4,'tensor_1'=2] {'tensor_0'}, use_global_device_ids=true, to_apply=%region_18.0 | all-reduce | flops 2 | bytes 16 | tf_op jit(solution)/shard_map/psum | solution.py:55
  566.6 5.9 %all-reduce.4 = (f32[]{:T(128)}, f32[]{:T(128)}) all-reduce(f32[]{:T(128)} %get-tuple-element.7, f32[]{:T(128)} %get-tuple-element.8), channel_id=1, replica_groups=mesh['dp_0'=16,'dp_1'=2,'dp_2'=2,'tensor_0'=4,'tensor_1'=2] {'tensor_1'}, use_global_device_ids=true, to_apply=%region_19.0 | all-reduce | flops 2 | bytes 16 | tf_op jit(solution)/shard_map/psum | solution.py:55
  573.8 0.6 broadcast_multiply_fusion
  (5 shorter events, 0.1 us)
Async XLA Ops:
  7.2 123.1 %copy-start = (bf16[1536,256]{1,0:T(8,128)(2,1)S(1)}, bf16[1536,256]{1,0:T(8,128)(2,1)}, u32[]{:S(2)}) copy-start(bf16[1536,256]{1,0:T(8,128)(2,1)} %param.5) | copy-start | bytes 2359300
  7.2 123.1 %all-gather.8.cloned.1.call-start = ((), (), s32[]{:S(2)}) async-start(), calls=%async_computation.5 | async-start | bytes 7077888 | tf_op jit(solution)/shard_map/all_gather | solution.py:76
  7.9 298.2 %all-gather.12.cloned.1.call-start = ((), (), s32[]{:S(2)}) async-start(), calls=%async_computation.7 | async-start | bytes 1114112 | tf_op jit(solution)/shard_map/all_gather | solution.py:33
  252.4 84.7 %all-gather.14.cloned.1.call-start = ((), (), s32[]{:S(2)}) async-start(), calls=%async_computation.8 | async-start | bytes 3145728 | tf_op jit(solution)/shard_map/all_gather | solution.py:33
  340.3 36.5 %all-to-all-start.1 = ((f32[8,256,256]{2,1,0:T(8,128)}), f32[8,256,256]{2,1,0:T(8,128)S(1)}, u32[]{:S(2)}, u32[]{:S(2)}) async-start(f32[8,256,256]{2,1,0:T(8,128)} %bitcast.7), calls=%async_computation.1 | async-start | bytes 4194304 | tf_op jit(solution)/shard_map/all_to_all | solution.py:92
  345.7 171.2 %all-gather.10.cloned.1.call-start = ((), (), s32[]{:S(2)}) async-start(), calls=%async_computation.6 | async-start | bytes 1064960 | tf_op jit(solution)/shard_map/all_gather | solution.py:122
  376.8 1.3 copy-start.1
  382.0 12.9 %copy-start.4 = (f32[32,256]{1,0:T(8,128)S(1)}, f32[32,256]{1,0:T(8,128)}, u32[]{:S(2)}) copy-start(f32[32,256]{1,0:T(8,128)} %param.7) | copy-start | bytes 98308
  382.0 12.9 %copy-start.5 = (f32[32,256]{1,0:T(8,128)S(1)}, f32[32,256]{1,0:T(8,128)}, u32[]{:S(2)}) copy-start(f32[32,256]{1,0:T(8,128)} %param.6) | copy-start | bytes 98308
  396.1 67.7 %copy-start.2 = (f32[32,256]{1,0:T(8,128)}, f32[32,256]{1,0:T(8,128)S(1)}, u32[]{:S(2)}) copy-start(f32[32,256]{1,0:T(8,128)S(1)} %get-tuple-element.28) | copy-start | bytes 98308
  396.1 67.7 %copy-start.3 = (f32[32,256]{1,0:T(8,128)}, f32[32,256]{1,0:T(8,128)S(1)}, u32[]{:S(2)}) copy-start(f32[32,256]{1,0:T(8,128)S(1)} %get-tuple-element.24) | copy-start | bytes 98308
  396.9 63.4 %all-to-all-start.3 = ((f32[8,32,256]{2,1,0:T(8,128)}), f32[8,32,256]{2,1,0:T(8,128)S(1)}, u32[]{:S(2)}, u32[]{:S(2)}) async-start(f32[8,32,256]{2,1,0:T(8,128)} %broadcast_in_dim.4), calls=%async_computation.3 | async-start | bytes 524288 | tf_op jit(solution)/shard_map/all_to_all | solution.py:61
  463.8 12.0 %all-to-all-start.4 = ((f32[8,32,256]{2,1,0:T(8,128)}), f32[8,32,256]{2,1,0:T(8,128)S(1)}, u32[]{:S(2)}, u32[]{:S(2)}) async-start(f32[8,32,256]{2,1,0:T(8,128)} %broadcast_in_dim.5), calls=%async_computation.4 | async-start | bytes 524288 | tf_op jit(solution)/shard_map/all_to_all | solution.py:61
Sparse Core Ops, SparseCore 0:
  11.1 119.1 all-gather.7
  252.6 53.5 all-gather.11
  308.2 28.8 all-gather.13
  396.3 120.6 all-gather.9
where the time goes:
time: 584 us; the launch traced here: 581 us
  waiting for transfers between devices  282 us (48%)
  blocking collectives  242 us (41%)
  between operations  16.6 us (3%)
  matrix products  15.5 us (3%)
  starting transfers between devices  13.6 us (2%)
  local copies, waits for them, and re-layouts  7.96 us (1%)
    all_to_all x2, blocking collectives, sum_at_owner(): blocks = lax.all_to_all(in_blocks(x, dim, length), axis, 0, 0, tiled=True)  125 us
    all_gather x1, waiting for transfers between devices, local(): lax.all_gather(activations, TENSOR, axis=1, tiled=True)  122 us
    psum x10, blocking collectives, by_axis(): x = lax.psum(x, axis)  112 us
    all_gather x2, waiting for transfers between devices, gather_in_order(): blocks = lax.all_gather(blocks, axes[k])  84.6 us
    all_gather x1, waiting for transfers between devices, local(): lax.all_gather(right_new.astype(jnp.bfloat16), DP, axis=0, tiled=True)  41.2 us
    all_to_all x1, waiting for transfers between devices, local(): lax.all_to_all(grad_cols, TENSOR, split_axis=0, concat_axis=1, tiled=True)  27.4 us
  transfers between devices with their start and end apart: 7, of which 6 were waited for; matrix products, arithmetic and copies ran while one was open for 2% of the time, Pallas kernels for 0%

commit v1 on v0

v1 whole, which is shorter than its diff:
```python
import jax
import jax.numpy as jnp
from jax import lax
from jax.experimental import pallas as pl
from jax.experimental.pallas import tpu as pltpu
from jax.sharding import Mesh
from jax.sharding import PartitionSpec as P

DP = ("z", "yl", "c")
TENSOR = ("x", "yh")
MESH = pl.DeviceIdType.MESH
F32 = jnp.float32
NEAR = (1, 15, 2)
BLOCKS = (0, 3, 1, 2)
TOKENS = 1536
HALF = 768
B = 2048


def dot(a, b, dims):
    return lax.dot_general(
        a, b, (dims, ((), ())), precision=lax.Precision.HIGHEST, preferred_element_type=F32
    )


def by_rows(a, b):
    return dot(a, b, ((1,), (1,)))


def by_columns(a, b):
    return dot(a.T, b, ((1,), (0,)))


def total(v):
    return jnp.sum(jnp.sum(v * v, axis=1, keepdims=True), axis=0, keepdims=True)


def kernel(
    a_ref, o_ref, ls_ref, rs_ref, left_ref, right_ref, update_ref,
    a_in, o_in, part, c_in, c_sum, y_in, tile, z1_in, z1_sum, z2_in, piece, grad, gz, stat,
    ls_in, hl, st, st_in, st_sum, qg, qg_in, ur, ur_in, la, turned, ub, uz, su, su_in, qu, qu_in,
    pr, pr_in, q_sum, qa, s_own, s1_in, s1_sum, s2_in,
    a_send, a_recv, send, recv, c_send, c_recv, y_send, y_recv, z_send, z_recv, ga_recv,
):
    z, yl, c = lax.axis_index("z"), lax.axis_index("yl"), lax.axis_index("c")
    x, yh = lax.axis_index("x"), lax.axis_index("yh")
    zh, zb, z1 = z // 4, z % 2, (z // 2) % 2
    ylc = 2 * yl + c
    place = ylc * 8 + x * 2 + yh

    def at(**other):
        return {**dict(z=z, yl=yl, c=c, x=x, yh=yh), **other}

    def x_peer(k):
        return at(x=lax.rem(x + k, 4))

    def z_peer(k):
        return at(z=lax.rem(z + k, 16))

    def flip(n, bit):
        return n + bit - 2 * n * bit

    def y_peer(d, **other):
        return at(c=flip(c, d % 2), yl=flip(yl, d // 2 % 2), yh=flip(yh, d // 4), **other)

    def plane_peer(d):
        bits = [flip((place >> i) % 2, (d >> i) % 2) for i in range(5)]
        return at(yh=bits[0], x=bits[1] + 2 * bits[2], c=bits[3], yl=bits[4])

    def remote(src, dst, s, r, peer):
        return pltpu.make_async_remote_copy(
            src_ref=src, dst_ref=dst, send_sem=s, recv_sem=r, device_id=peer, device_id_type=MESH
        )

    def settle(view, sem):
        pltpu.make_async_copy(view, view, sem).wait()

    barrier = pltpu.get_barrier_semaphore()

    def greet(peer):
        pl.semaphore_signal(barrier, inc=1, device_id=peer, device_id_type=MESH)

    def greet_plane(d, _):
        greet(plane_peer(d))
        return _

    def greet_column(k, _):
        greet(z_peer(k))
        greet(at(z=lax.rem(z + k, 16), yh=1 - yh))
        return _

    lax.fori_loop(1, 32, greet_plane, 0)
    lax.fori_loop(1, 16, greet_column, 0)
    z_pair = z + 2 - 4 * z1
    for d in (1, 2, 3, 5, 6, 7):
        greet(y_peer(d, z=z_pair))
    pl.semaphore_wait(barrier, 31 + 30 + 6)

    remote(o_ref, o_in, send.at[0], recv.at[0], at(yh=1 - yh)).start()

    def rows(h):
        return pl.ds(h * HALF, HALF)

    for slot, k, h in ((0, 1, 0), (1, 3, 1), (0, 1, 1), (1, 3, 0)):
        remote(
            a_ref.at[rows(h)], a_in.at[slot, rows(h)], a_send, a_recv.at[slot, h], x_peer(k)
        ).start()

    stat_to = stat.at[zh, zb, :, pl.ds(pl.multiple_of(yh * 256, 256), 256)]

    def send_stat(k, _):
        remote(rs_ref, stat_to, send.at[1], recv.at[1], at(z=lax.rem(z + k, 16), yh=z1)).start()
        return _

    lax.fori_loop(1, 16, send_stat, 0)
    own_stat = remote(rs_ref, stat_to, send.at[2], recv.at[1], at(yh=z1))
    pl.when(z1 == yh)(lambda: pltpu.make_async_copy(rs_ref, stat_to, recv.at[1]).start())
    pl.when(z1 != yh)(lambda: own_stat.start())
    ls_sends = []
    for b in range(2):
        zt = 4 * x + 2 * yh + b
        ls_from, ls_to = ls_ref.at[:, pl.ds(b * 128, 128)], ls_in.at[zh, zb]
        go = remote(ls_from, ls_to, send.at[3 + b], recv.at[2], at(z=zt, yh=z1))
        ls_sends.append((zt, go))

        def keep(ls_from=ls_from, ls_to=ls_to):
            pltpu.make_async_copy(ls_from, ls_to, recv.at[2]).start()

        pl.when(zt == z)(keep)
        pl.when(zt != z)(go.start)

    own_cols = pl.ds(pl.multiple_of(yh * 256, 256), 256)
    other_cols = pl.ds(pl.multiple_of((1 - yh) * 256, 256), 256)

    def terms(k, own):
        acts = a_ref[...] if k == 0 else a_in[k - 1]
        block = lax.dot_general(
            acts,
            o_ref[...] if own else o_in[...],
            (((0,), (0,)), ((), ())),
            preferred_element_type=F32,
        )
        part[k, :, :, :, :, own_cols if own else other_cols] = block.reshape(2, 2, 2, 32, 256)

    def block_of(k):
        return lax.rem(x + BLOCKS[k], 4)

    def c_start(k):
        remote(part.at[k, :, :, 1 - c], c_in.at[k], c_send.at[k], c_recv.at[k], at(c=1 - c)).start()

    def c_end(k):
        settle(c_in.at[k], c_recv.at[k])
        c_sum[k] = part[k, :, :, c] + c_in[k]
        remote(c_sum.at[k, :, 1 - yl], y_in.at[k], y_send.at[k], y_recv.at[k], at(yl=1 - yl)).start()

    def half_of(zz):
        return pl.ds(pl.multiple_of(flip((zz // 2) % 2, yh) * 16, 16), 16)

    def y_end(k):
        settle(y_in.at[k], y_recv.at[k])
        tile[k] = c_sum[k, :, yl] + y_in[k]
        for i, step in enumerate(NEAR):
            m = lax.rem(z + step, 16)
            remote(
                tile.at[k, m % 2, half_of(m)], z1_in.at[k, i], z_send.at[k], z_recv.at[k], z_peer(step)
            ).start()

    def z1_end(k):
        settle(z1_in.at[k], z_recv.at[k])
        z1_sum[k] = tile[k, zb, half_of(z)] + z1_in[k, 0] + z1_in[k, 1] + z1_in[k, 2]
        xb = block_of(k)
        far = lax.rem(xb - zh + 4, 4)

        def away():
            remote(
                z1_sum.at[k], z2_in.at[far - 1], send.at[5], recv.at[3], at(z=4 * xb + z % 4)
            ).start()

        def stay():
            piece[...] = z1_sum[k]

        pl.when(far != 0)(away)
        pl.when(far == 0)(stay)

    terms(0, True)
    settle(a_in.at[0, rows(0)], a_recv.at[0, 0])
    remote(a_in.at[0, rows(0)], a_in.at[2, rows(0)], a_send, a_recv.at[2, 0], x_peer(1)).start()
    settle(a_in.at[1, rows(1)], a_recv.at[1, 1])
    remote(a_in.at[1, rows(1)], a_in.at[2, rows(1)], a_send, a_recv.at[2, 1], x_peer(3)).start()
    settle(o_in, recv.at[0])
    terms(0, False)
    c_start(0)
    settle(a_in.at[0, rows(1)], a_recv.at[0, 1])
    terms(1, True)
    terms(1, False)
    c_start(1)
    c_end(0)
    settle(a_in.at[1, rows(0)], a_recv.at[1, 0])
    terms(2, True)
    terms(2, False)
    c_start(2)
    c_end(1)
    y_end(0)

    @pl.when(x == zh)
    def _():
        settle(ls_in, recv.at[2])
        for k in range(1, 4):
            remote(ls_in, hl.at[1], send.at[6], recv.at[4], x_peer(k)).start()
        pltpu.make_async_copy(ls_in, hl.at[1], recv.at[4]).start()

    settle(a_in.at[2, rows(0)], a_recv.at[2, 0])
    settle(a_in.at[2, rows(1)], a_recv.at[2, 1])
    terms(3, True)
    terms(3, False)
    c_start(3)
    c_end(2)
    y_end(1)
    z1_end(0)
    c_end(3)
    y_end(2)
    z1_end(1)
    y_end(3)
    z1_end(2)
    z1_end(3)
    settle(z2_in, recv.at[3])
    piece[...] = piece[...] + z2_in[0] + z2_in[1] + z2_in[2]

    mine = half_of(z)
    grad[zh, zb, mine] = piece[...]
    home = 4 * zh + 2 * yh + zb
    gz_rows = gz.at[pl.ds(pl.multiple_of(ylc * 32 + flip(z1, yh) * 16, 16), 16)]
    for i, step in enumerate((4, 12, 8)):
        remote(piece, grad.at[zh, zb, mine], send.at[7], ga_recv.at[i], z_peer(step)).start()
    for step in NEAR:
        remote(piece, grad.at[zh, zb, mine], send.at[8], recv.at[5], z_peer(step)).start()
    for d in range(1, 8):
        remote(piece, gz_rows, send.at[9], recv.at[6], y_peer(d, z=home)).start()
    gz_send = remote(piece, gz_rows, send.at[10], recv.at[6], at(z=home))
    pl.when(home == z)(lambda: pltpu.make_async_copy(piece, gz_rows, recv.at[6]).start())
    pl.when(home != z)(lambda: gz_send.start())
    for i, step in enumerate((4, 12, 8)):
        zs = lax.rem(zh + 4 - step // 4, 4)
        view = grad.at[zs, zb, mine]
        settle(view, ga_recv.at[i])
        for step2 in NEAR:
            remote(view, view, send.at[11], recv.at[5], z_peer(step2)).start()

    settle(gz, recv.at[6])
    settle(stat, recv.at[1])
    rows_z = gz[...]
    qg[...] = by_rows(stat[...].reshape(256, 512), rows_z).reshape(4, 64, 128)
    for k in range(1, 4):
        to = lax.rem(x + k, 4)
        remote(qg.at[to], qg_in.at[k - 1], send.at[12], recv.at[7], x_peer(k)).start()
    settle(grad.at[pl.ds(0, 3)], recv.at[5])

    @pl.when(x == zh)
    def _():
        cols = grad.at[:, :, :, pl.ds(pl.multiple_of(z % 4 * 128, 128), 128)]
        for k in range(1, 4):
            remote(cols, hl.at[0], send.at[13], recv.at[8], x_peer(k)).start()
        pltpu.make_async_copy(cols, hl.at[0], recv.at[8]).start()

    def tile_of():
        return grad[...].reshape(256, 512)

    st[...] = by_rows(tile_of(), rows_z)
    for k in range(1, 4):
        remote(st, st_in.at[k - 1], send.at[14], recv.at[9], x_peer(k)).start()
    settle(hl.at[0], recv.at[8])
    settle(hl.at[1], recv.at[4])
    ur[1] = by_columns(hl[0].reshape(256, 128), tile_of())
    settle(st_in, recv.at[9])
    st_sum[...] = st[...] + (st_in[0] + st_in[1] + st_in[2])
    lt = 0.9 * hl[1].reshape(256, 128) + 0.1 * st_sum[...]
    turned[...] = lt
    ur[0] = by_columns(lt, tile_of())

    def block_at(ref, d, *lead):
        r = pl.multiple_of((flip(c, d % 2) + 2 * flip(yl, d // 2 % 2)) * 32, 32)
        col = pl.multiple_of(flip(yh, d // 4) * 256, 256)
        return ref.at[(*lead, pl.ds(r, 32), pl.ds(col, 256))]

    for d in range(1, 8):
        remote(
            block_at(ur, d, slice(None)), ur_in.at[d - 1], send.at[15], recv.at[10], y_peer(d)
        ).start()
    own = turned[pl.ds(pl.multiple_of(x * 64, 64), 64), :]
    la[ylc] = own
    for d in range(1, 4):
        remote(la.at[ylc], la.at[ylc], send.at[16], recv.at[11], y_peer(d)).start()
    left_sq = total(own)
    grad_sq = total(piece[...])

    settle(ur_in, recv.at[10])
    u_block = block_at(ur, 0, 0)[...]
    r_block = block_at(ur, 0, 1)[...]
    for d in range(7):
        u_block = u_block + ur_in[d, 0]
        r_block = r_block + ur_in[d, 1]
    ub[...] = u_block
    block_at(uz, 0)[...] = u_block
    for d in range(1, 8):
        remote(ub, block_at(uz, 0), send.at[17], recv.at[12], y_peer(d)).start()
    right = 0.9 * rs_ref[...] + 0.1 * r_block
    right_ref[...] = right
    right_sq = total(right)
    lane = lax.broadcasted_iota(jnp.int32, (8, 128), 1)

    def sum_in_plane(n, values):
        v = jnp.zeros((8, 128), F32)
        for i, value in enumerate(values):
            v = jnp.where(lane == i, value, v)
        s_own[n] = v

        def out(d, _):
            remote(s_own.at[n], s1_in.at[n, d - 1], send.at[18 + n], recv.at[13 + n], plane_peer(d)).start()
            return _

        lax.fori_loop(1, 32, out, 0)

    def sum_along_z(n):
        settle(s1_in.at[n], recv.at[13 + n])
        s1_sum[n] = s_own[n] + jnp.sum(s1_in[n], axis=0)

        def out(k, _):
            remote(s1_sum.at[n], s2_in.at[n, k - 1], send.at[20 + n], recv.at[15 + n], z_peer(k)).start()
            return _

        lax.fori_loop(1, 16, out, 0)

    def sums(n, count):
        settle(s2_in.at[n], recv.at[15 + n])
        v = s1_sum[n] + jnp.sum(s2_in[n], axis=0)
        first = lax.broadcasted_iota(jnp.int32, (8, 128), 0) == 0
        picked = [jnp.where((lane == i) & first, v, 0.0) for i in range(count)]
        return [jnp.sum(jnp.sum(p, axis=1, keepdims=True), axis=0, keepdims=True) for p in picked]

    sum_in_plane(0, (left_sq, right_sq, grad_sq))

    settle(uz.at[pl.ds(0, 112)], recv.at[12])
    rows_u = uz[...]
    su[...] = by_rows(tile_of(), rows_u)
    for k in range(1, 4):
        remote(su, su_in.at[k - 1], send.at[22], recv.at[17], x_peer(k)).start()
    qu[...] = by_rows(stat[...].reshape(256, 512), rows_u).reshape(4, 64, 128)
    for k in range(1, 4):
        to = lax.rem(x + k, 4)
        remote(qu.at[to], qu_in.at[k - 1], send.at[23], recv.at[18], x_peer(k)).start()
    sum_along_z(0)

    def assembled(slots):
        v = slots[...].reshape(4, 2, 32, 128)
        whole = jnp.concatenate([v[i, b] for b in range(2) for i in range(4)], axis=0)
        return whole.T

    settle(la.at[pl.ds(0, 3)], recv.at[11])
    lt_rows = assembled(la)
    uz_rows = pl.ds(pl.multiple_of(ylc * 32, 32), 32)
    pr[:, 0:256] = lt_rows
    left_ref[...] = pr[uz_rows, 0:256]

    settle(su_in, recv.at[17])
    s_u = su[...] + (su_in[0] + su_in[1] + su_in[2])
    settle(qg_in, recv.at[7])
    settle(qu_in, recv.at[18])
    left_total, right_total, grad_total = sums(0, 3)
    left_scale = jnp.sqrt(left_total / B + 1e-06)
    right_scale = jnp.sqrt(right_total / B + 1e-06)
    q_g = qg[x] + qg_in[0] + qg_in[1] + qg_in[2]
    q_u = qu[x] + qu_in[0] + qu_in[1] + qu_in[2]
    q_sum[...] = 0.9 * (5.0 * q_g - q_u / left_scale)
    qa[ylc] = q_sum[...]
    for d in range(1, 4):
        remote(q_sum, qa.at[ylc], send.at[24], recv.at[19], y_peer(d)).start()
    pr[...] = by_columns(0.1 * (5.0 * st_sum[...] - s_u / left_scale), tile_of())
    for d in range(1, 8):
        remote(block_at(pr, d), pr_in.at[d - 1], send.at[25], recv.at[20], y_peer(d)).start()
    pre_left = 5.0 * block_at(gz, 0)[...] - ub[...] / left_scale
    settle(qa.at[pl.ds(0, 3)], recv.at[19])
    turned[pl.ds(0, 128), :] = assembled(qa)[:, 0:128]
    turned[pl.ds(128, 128), :] = assembled(qa)[:, 128:256]
    low = turned[pl.ds(pl.multiple_of(ylc * 32, 32), 32), :]
    high = turned[pl.ds(pl.multiple_of(128 + ylc * 32, 32), 32), :]
    product = jnp.concatenate([low, high], axis=1) + block_at(pr, 0)[...]
    settle(pr_in, recv.at[20])
    for d in range(7):
        product = product + pr_in[d]
    pre = 5.0 * pre_left - product / right_scale
    sum_in_plane(1, (total(pre),))
    sum_along_z(1)
    (pre_total,) = sums(1, 1)
    update_ref[...] = pre * (jnp.sqrt(grad_total + 1e-06) / jnp.sqrt(pre_total + 1e-06))

    settle(o_in, send.at[0])
    settle(a_in, a_send)
    settle(ur.at[:, pl.ds(0, 120)], send.at[1])
    pl.when(z1 != yh)(own_stat.wait_send)
    for zt, go in ls_sends:
        pl.when(zt != z)(go.wait_send)
    for k in range(4):
        settle(c_in.at[k], c_send.at[k])
        settle(y_in.at[k], y_send.at[k])
        settle(z1_in.at[k], z_send.at[k])
    settle(z2_in, send.at[5])
    settle(z2_in, send.at[7])
    settle(z2_in, send.at[8])
    settle(gz.at[pl.ds(0, 112)], send.at[9])
    pl.when(home != z)(gz_send.wait_send)
    settle(grad.at[pl.ds(0, 3), :, pl.ds(0, 24)], send.at[11])
    settle(qg_in, send.at[12])

    @pl.when(x == zh)
    def _():
        settle(st_in, send.at[6])
        settle(st_in, send.at[13])

    settle(st_in, send.at[14])
    settle(ur_in, send.at[15])
    settle(qg_in, send.at[16])
    settle(pr_in, send.at[17])
    for n in range(2):
        settle(s1_in.at[n], send.at[18 + n])
        settle(s2_in.at[n], send.at[20 + n])
    settle(st_in, send.at[22])
    settle(qg_in, send.at[23])
    settle(qg_in, send.at[24])
    settle(pr_in, send.at[25])


def local(activations, out_grads, left_stat, right_stat):
    vmem = pl.BlockSpec(memory_space=pltpu.VMEM)
    block = jax.ShapeDtypeStruct((32, 256), F32)
    bf16 = jnp.bfloat16
    shapes = [
        ((3, TOKENS, 256), bf16), ((TOKENS, 256), bf16),
        ((4, 2, 2, 2, 32, 512), F32), ((4, 2, 2, 32, 512), F32),
        ((4, 2, 2, 32, 512), F32), ((4, 2, 32, 512), F32),
        ((4, 2, 32, 512), F32), ((4, 3, 16, 512), F32),
        ((4, 16, 512), F32), ((3, 16, 512), F32), ((16, 512), F32),
        ((4, 2, 32, 512), F32), ((128, 512), F32), ((4, 2, 32, 512), F32),
        ((4, 2, 32, 128), F32), ((2, 4, 2, 32, 128), F32),
        ((256, 128), F32), ((3, 256, 128), F32), ((256, 128), F32),
        ((4, 64, 128), F32), ((3, 64, 128), F32),
        ((2, 128, 512), F32), ((7, 2, 32, 256), F32),
        ((4, 64, 128), F32), ((256, 128), F32), ((32, 256), F32), ((128, 512), F32),
        ((256, 128), F32), ((3, 256, 128), F32),
        ((4, 64, 128), F32), ((3, 64, 128), F32),
        ((128, 512), F32), ((7, 32, 256), F32),
        ((64, 128), F32), ((4, 64, 128), F32),
        ((2, 8, 128), F32), ((2, 31, 8, 128), F32),
        ((2, 8, 128), F32), ((2, 15, 8, 128), F32),
    ]
    dma = pltpu.SemaphoreType.DMA
    sems = [dma, dma((3, 2)), dma((26,)), dma((21,))] + [dma((4,))] * 6 + [dma((3,))]
    return pl.pallas_call(
        kernel,
        out_shape=(block, block, block),
        in_specs=[vmem] * 4,
        out_specs=(vmem, vmem, vmem),
        scratch_shapes=[pltpu.VMEM(s, d) for s, d in shapes] + sems,
        compiler_params=pltpu.CompilerParams(
            collective_id=0, has_side_effects=True, vmem_limit_bytes=58 * 2**20
        ),
        cost_estimate=pl.CostEstimate(flops=2 * 10**9, bytes_accessed=4 * 10**6, transcendentals=0),
    )(activations, out_grads, left_stat, right_stat)


def solution(mesh):
    finer = Mesh(mesh.devices.reshape(16, 2, 2, 4, 2), ("z", "yl", "c", "x", "yh"))
    spec = P(DP, TENSOR)
    return jax.shard_map(
        local,
        mesh=finer,
        in_specs=(spec,) * 4,
        out_specs=(spec,) * 3,
        check_vma=False,
    )
```

time: 584 us -> 158 us (0.27)
  waiting for transfers between devices: 282 us -> 0 us
  blocking collectives: 242 us -> 0 us
  Pallas kernels: 0 us -> 154 us
  between operations: 16.6 us -> 0.65 us
  matrix products: 15.5 us -> 0 us
  starting transfers between devices: 13.6 us -> 0 us
    all_gather x4 -> x0, waiting for transfers between devices: 248 us -> none  [the longest x1 122 us: local(): lax.all_gather(activations, TENSOR, axis=1, tiled=True)]
    pallas_call x0 -> x1, Pallas kernels: none -> 154 us  [local(): pl.pallas_call(kernel, out_shape=(block, block, block), in_specs=[vmem] *...]
    all_to_all x2 -> x0, blocking collectives: 125 us -> none  [sum_at_owner(): blocks = lax.all_to_all(in_blocks(x, dim, length), axis, 0, 0, tiled=True)]
    psum x10 -> x0, blocking collectives: 112 us -> none  [by_axis(): x = lax.psum(x, axis)]
    all_to_all x3 -> x0, waiting for transfers between devices: 33.5 us -> none  [the longest x1 27.4 us: local(): lax.all_to_all(grad_cols, TENSOR, split_axis=0, concat_axis=1, tiled=True)]
    dot_general x5 -> x0, matrix products: 15.5 us -> none  [the longest x1 4.74 us: local(): lax.dot_general(lax.all_gather(activations, TENSOR, axis=1, tiled=True),...]
    all_to_all x3 -> x0, starting transfers between devices: 13.5 us -> none  [the longest x2 8.05 us: sent_to_all(): lax.all_to_all(jnp.broadcast_to(x[None], (length, *x.shape)), axis, 0, 0,...]
  transfers between devices with their start and end apart: 7 -> 0, of which waited for: 6 -> 0; matrix products, arithmetic and copies ran while one was open for 2% -> 0% of each run, Pallas kernels for 0% -> 0%
where the time goes in v1:
time: 158 us
  Pallas kernels  154 us (97%)
  local copies, waits for them, and re-layouts  2.77 us (2%)
    pallas_call x1, Pallas kernels, local(): pl.pallas_call(kernel, out_shape=(block, block, block), in_specs=[vmem] *...  154 us

profile of v1, /device:TPU:1, one launch (start us, length us, event | category | flops | bytes accessed | tf_op | source)
XLA Modules:
  0.0 157.8 jit_solution(10755803283519703476)
XLA Ops:
  0.6 154.4 %shard_map.67 = (f32[32,256]{1,0:T(8,128)}, f32[32,256]{1,0:T(8,128)}, f32[32,256]{1,0:T(8,128)}) custom-call(bf16[1536,256]{1,0:T(8,128)(2,1)} %a_ref.1, bf16[1536,256]{1,0:T(8,128)(2,1)} %o_ref.1, f32[32,256]{1,0:T(8,128)} %ls_ref.1, f32[32,256]{1,0:T(8,128)} %rs_ref.1), custom_call_target="tpu_custom_call" | custom-call | flops 2000000000 | bytes 4000000 | tf_op jit(solution)/shard_map/pallas_call | solution.py:457
  155.0 0.0 copy-start.1
  155.0 1.4 copy.10
  156.4 0.0 copy-done.1
  156.4 0.0 copy-start
  156.4 0.6 copy.11
  157.0 0.2 copy-done
  157.2 0.6 copy.12
Async XLA Ops:
  155.0 1.4 copy-start.1
  156.4 0.8 copy-start

commit v2 on v1

v2 whole, which is shorter than its diff:
```python
import jax
import jax.numpy as jnp
from jax import lax
from jax.experimental import pallas as pl
from jax.experimental.pallas import tpu as pltpu
from jax.sharding import Mesh
from jax.sharding import PartitionSpec as P

DP = ("z", "yl", "c")
TENSOR = ("x", "yh")
MESH = pl.DeviceIdType.MESH
F32 = jnp.float32
NEAR = (1, 15, 2)
FAR = (4, 12, 8)
DIRECT = (3,)
BLOCKS = (0, 3, 1, 2)
TOKENS = 1536
HALF = 768
B = 2048


def dot(a, b, dims):
    return lax.dot_general(a, b, (dims, ((), ())), preferred_element_type=F32)


def parts(v):
    high = v.astype(jnp.bfloat16)
    return high, (v - high.astype(F32)).astype(jnp.bfloat16)


def by_rows(a, b):
    high, low = parts(b)
    over = ((1,), (1,))
    small = dot(a[0], low, over)
    if len(a) == 2:
        small = small + dot(a[1], high, over)
    return dot(a[0], high, over) + small


def by_columns(a, b):
    high, low = parts(a.T)
    over = ((1,), (0,))
    return dot(high, b[0], over) + (dot(low, b[0], over) + dot(high, b[1], over))


def total(v):
    return jnp.sum(jnp.sum(v * v, axis=1, keepdims=True), axis=0, keepdims=True)


def kernel(
    a_ref, o_ref, ls_ref, rs_ref, left_ref, right_ref, update_ref,
    a_own, o_own, a_in, o_in, part, c_in, c_sum, y_in, tile, z1_in, z1_sum, z2_in, grad, g_parts, gz, stat, rs_half,
    ls_in, hl, st, st_in, st_sum, qg, qg_in, ur, ur_in, la, turned, ub, uz, su, su_in, qu, qu_in,
    pr, pr_in, q_sum, qa, s_own, s1_in, s1_sum, s2_in,
    a_send, a_recv, send, recv, c_send, c_recv, y_send, y_recv, z_send, z_recv, z2_send, z2_recv,
    far_send, far_recv, near_send, near_recv, s_sems, relay,
):
    z, yl, c = lax.axis_index("z"), lax.axis_index("yl"), lax.axis_index("c")
    x, yh = lax.axis_index("x"), lax.axis_index("yh")
    zh, zb, z1 = z // 4, z % 2, (z // 2) % 2
    ylc = 2 * yl + c
    place = ylc * 8 + x * 2 + yh

    def at(**other):
        return {**dict(z=z, yl=yl, c=c, x=x, yh=yh), **other}

    def x_peer(k):
        return at(x=lax.rem(x + k, 4))

    def z_peer(k):
        return at(z=lax.rem(z + k, 16))

    def flip(n, bit):
        return n + bit - 2 * n * bit

    def y_peer(d, **other):
        return at(c=flip(c, d % 2), yl=flip(yl, d // 2 % 2), yh=flip(yh, d // 4), **other)

    bits = [(yh, 1 - yh), None, None, (c, 1 - c), (yl, 1 - yl)]
    xs = [flip(x % 2, k % 2) + 2 * flip(x // 2, k // 2) for k in range(4)]

    def plane_peer(d):
        return at(yh=bits[0][d % 2], x=xs[d // 2 % 4], c=bits[3][d // 8 % 2], yl=bits[4][d // 16])

    def remote(src, dst, s, r, peer):
        return pltpu.make_async_remote_copy(
            src_ref=src, dst_ref=dst, send_sem=s, recv_sem=r, device_id=peer, device_id_type=MESH
        )

    def settle(view, sem):
        pltpu.make_async_copy(view, view, sem).wait()

    drain = []

    def sent(view, sem):
        drain.append(lambda: settle(view, sem))

    barrier = pltpu.get_barrier_semaphore()

    def greet(peer):
        pl.semaphore_signal(barrier, inc=1, device_id=peer, device_id_type=MESH)

    copies = [
        pltpu.make_async_copy(a_ref, a_own, send.at[7]),
        pltpu.make_async_copy(o_ref, o_own, send.at[8]),
    ]
    for copy in copies:
        copy.start()
    for d in range(1, 32):
        greet(plane_peer(d))
    for k in (1, 2, 14, 15):
        greet(z_peer(k))
    pl.semaphore_wait(barrier, 31 + 4)

    def tell(n, k):
        pl.semaphore_signal(relay.at[n], inc=1, device_id=z_peer(k), device_id_type=MESH)

    remote(o_ref, o_in, send.at[11], recv.at[0], at(yh=1 - yh)).start()
    sent(o_in, send.at[11])
    sent(a_in, a_send)

    def rows(h):
        return pl.ds(h * HALF, HALF)

    for slot, k, h in ((0, 1, 0), (1, 3, 1), (0, 1, 1), (1, 3, 0)):
        remote(
            a_ref.at[rows(h)], a_in.at[slot, rows(h)], a_send, a_recv.at[slot, h], x_peer(k)
        ).start()

    for k in (1, 2, 14, 15):
        tell(0, k)

    own_cols = pl.ds(pl.multiple_of(yh * 256, 256), 256)
    other_cols = pl.ds(pl.multiple_of((1 - yh) * 256, 256), 256)

    def terms(k, own):
        acts = a_own[...] if k == 0 else a_in[k - 1]
        block = lax.dot_general(
            acts,
            o_own[...] if own else o_in[...],
            (((0,), (0,)), ((), ())),
            preferred_element_type=F32,
        )
        part[k, :, :, :, :, own_cols if own else other_cols] = block.reshape(2, 2, 2, 32, 256)

    def block_of(k):
        return lax.rem(x + BLOCKS[k], 4)

    def c_start(k):
        remote(part.at[k, :, :, 1 - c], c_in.at[k], c_send.at[k], c_recv.at[k], at(c=1 - c)).start()
        sent(c_in.at[k], c_send.at[k])

    def c_end(k):
        settle(c_in.at[k], c_recv.at[k])
        c_sum[k] = part[k, :, :, c] + c_in[k]
        remote(c_sum.at[k, :, 1 - yl], y_in.at[k], y_send.at[k], y_recv.at[k], at(yl=1 - yl)).start()
        sent(y_in.at[k], y_send.at[k])

    def half_of(zz):
        return pl.ds(pl.multiple_of(flip((zz // 2) % 2, yh) * 16, 16), 16)

    def y_end(k):
        settle(y_in.at[k], y_recv.at[k])
        tile[k] = c_sum[k, :, yl] + y_in[k]
        for i, step in enumerate(NEAR):
            m = lax.rem(z + step, 16)
            remote(
                tile.at[k, m % 2, half_of(m)], z1_in.at[k, i], z_send.at[k], z_recv.at[k], z_peer(step)
            ).start()
        sent(z1_in.at[k], z_send.at[k])

    mine = half_of(z)

    def columns_of(zz):
        return pl.ds(pl.multiple_of(zz * 128, 128), 128)

    def z1_end(k):
        settle(z1_in.at[k], z_recv.at[k])
        z1_sum[k] = tile[k, zb, mine] + z1_in[k, 0] + z1_in[k, 1] + z1_in[k, 2]
        if k in DIRECT:
            for i, step in enumerate(FAR):
                remote(z1_sum.at[k], z2_in.at[k, i], z2_send.at[k], z2_recv.at[k], z_peer(step)).start()
            sent(z2_in.at[k], z2_send.at[k])
            return
        for i, step in enumerate(FAR):
            at_zh = columns_of(lax.rem(zh + step // 4, 4))
            remote(
                z1_sum.at[k, :, at_zh], z2_in.at[k, i, :, at_zh], z2_send.at[k], z2_recv.at[k], z_peer(step)
            ).start()
        sent(z2_in.at[k, :, :, pl.ds(0, 128)], z2_send.at[k])

    def piece_of(k):
        return grad.at[block_of(k), zb, mine]

    def z2_own(k):
        if k in DIRECT:
            return
        settle(z2_in.at[k, :, :, pl.ds(0, 128)], z2_recv.at[k])
        cols = columns_of(zh)
        mine_k = grad.at[block_of(k), zb, mine, cols]
        mine_k[...] = z1_sum[k, :, cols] + (z2_in[k, 0, :, cols] + z2_in[k, 1, :, cols] + z2_in[k, 2, :, cols])
        for step in FAR:
            remote(mine_k, mine_k, far_send.at[k], far_recv.at[k], z_peer(step)).start()
        sent(z2_in.at[k, :, :, pl.ds(0, 128)], far_send.at[k])

    def z2_end(k):
        if k in DIRECT:
            settle(z2_in.at[k], z2_recv.at[k])
            piece_of(k)[...] = z1_sum[k] + (z2_in[k, 0] + z2_in[k, 1] + z2_in[k, 2])
        else:
            settle(z2_in.at[k, :, :, pl.ds(0, 128)], far_recv.at[k])
        for step in NEAR:
            remote(piece_of(k), piece_of(k), near_send.at[k], near_recv.at[k], z_peer(step)).start()
        sent(z2_in.at[k], near_send.at[k])

    def z3_end(k):
        settle(z2_in.at[k], near_recv.at[k])
        xb = block_of(k)
        high, low = parts(grad[xb].reshape(64, 512))
        g_parts[0, xb] = high
        g_parts[1, xb] = low

    rs_half[...] = rs_ref[...].astype(jnp.bfloat16)
    for copy in copies:
        copy.wait()
    terms(0, True)
    pl.semaphore_wait(relay.at[0], 4)
    for k in (3, 4, 12, 13):
        tell(1, k)
    settle(a_in.at[0, rows(0)], a_recv.at[0, 0])
    remote(a_in.at[0, rows(0)], a_in.at[2, rows(0)], a_send, a_recv.at[2, 0], x_peer(1)).start()
    settle(a_in.at[1, rows(1)], a_recv.at[1, 1])
    remote(a_in.at[1, rows(1)], a_in.at[2, rows(1)], a_send, a_recv.at[2, 1], x_peer(3)).start()
    pl.semaphore_wait(relay.at[1], 4)
    tell(2, 4)
    tell(2, 12)

    pl.semaphore_wait(relay.at[2], 2)

    stat_to = stat.at[zh, zb, :, pl.ds(pl.multiple_of(yh * 256, 256), 256)]
    for step in FAR:
        remote(rs_half, stat_to, send.at[1], recv.at[1], at(z=lax.rem(z + step, 16), yh=z1)).start()
    own_stat = remote(rs_half, stat_to, send.at[2], recv.at[1], at(yh=z1))
    pl.when(z1 == yh)(lambda: pltpu.make_async_copy(rs_half, stat_to, recv.at[1]).start())
    pl.when(z1 != yh)(lambda: own_stat.start())
    sent(stat.at[pl.ds(0, 3), 0, :, pl.ds(0, 256)], send.at[1])
    drain.append(lambda: pl.when(z1 != yh)(own_stat.wait_send))
    for b in range(2):
        zt = 4 * x + 2 * yh + b
        ls_from, ls_to = ls_ref.at[:, pl.ds(b * 128, 128)], ls_in.at[zh, zb]
        go = remote(ls_from, ls_to, send.at[3 + b], recv.at[2], at(z=zt, yh=z1))
        drain.append(lambda zt=zt, go=go: pl.when(zt != z)(go.wait_send))

        def keep(ls_from=ls_from, ls_to=ls_to):
            pltpu.make_async_copy(ls_from, ls_to, recv.at[2]).start()

        pl.when(zt == z)(keep)
        pl.when(zt != z)(go.start)

    settle(o_in, recv.at[0])
    terms(0, False)
    c_start(0)
    settle(a_in.at[0, rows(1)], a_recv.at[0, 1])
    terms(1, True)
    terms(1, False)
    c_start(1)

    @pl.when(z1 == yh)
    def _():
        view = stat.at[:, zb]
        settle(view, recv.at[1])
        for step in NEAR:
            remote(view, view, send.at[5], recv.at[3], z_peer(step)).start()

    drain.append(lambda: pl.when(z1 == yh)(lambda: settle(z2_in, send.at[5])))

    c_end(0)
    settle(a_in.at[1, rows(0)], a_recv.at[1, 0])
    terms(2, True)
    terms(2, False)
    c_start(2)
    c_end(1)
    c_end(2)
    y_end(0)

    settle(a_in.at[2, rows(0)], a_recv.at[2, 0])
    settle(a_in.at[2, rows(1)], a_recv.at[2, 1])
    terms(3, True)
    terms(3, False)
    c_start(3)

    @pl.when(x == zh)
    def _():
        settle(ls_in, recv.at[2])
        for k in range(1, 4):
            remote(ls_in, hl.at[1], send.at[6], recv.at[4], x_peer(k)).start()
        pltpu.make_async_copy(ls_in, hl.at[1], recv.at[4]).start()

    drain.append(lambda: pl.when(x == zh)(lambda: settle(st_in, send.at[6])))

    y_end(1)
    z1_end(0)
    c_end(3)
    y_end(2)
    z1_end(1)
    y_end(3)
    z1_end(2)
    z2_own(0)
    z1_end(3)
    z2_own(1)
    z2_own(2)
    z2_end(0)
    z2_end(1)
    z2_own(3)
    z2_end(2)
    z3_end(0)
    z2_end(3)

    home = 4 * zh + 2 * yh + zb
    gz_rows = gz.at[pl.ds(pl.multiple_of(ylc * 32 + flip(z1, yh) * 16, 16), 16)]
    piece = grad.at[zh, zb, mine]
    for d in range(1, 8):
        remote(piece, gz_rows, send.at[9], recv.at[6], y_peer(d, z=home)).start()
    gz_send = remote(piece, gz_rows, send.at[10], recv.at[6], at(z=home))
    pl.when(home == z)(lambda: pltpu.make_async_copy(piece, gz_rows, recv.at[6]).start())
    pl.when(home != z)(lambda: gz_send.start())
    sent(gz.at[pl.ds(0, 112)], send.at[9])
    drain.append(lambda: pl.when(home != z)(gz_send.wait_send))
    z3_end(1)
    z3_end(2)
    z3_end(3)
    settle(gz, recv.at[6])
    rows_z = gz[...]

    def tile_of():
        return g_parts[0].reshape(256, 512), g_parts[1].reshape(256, 512)

    st[...] = by_rows(tile_of(), rows_z)
    for k in range(1, 4):
        remote(st, st_in.at[k - 1], send.at[14], recv.at[9], x_peer(k)).start()
    sent(st_in, send.at[14])

    @pl.when(x == zh)
    def _():
        cols = grad.at[:, :, :, pl.ds(pl.multiple_of(z % 4 * 128, 128), 128)]
        for k in range(1, 4):
            remote(cols, hl.at[0], send.at[13], recv.at[8], x_peer(k)).start()
        pltpu.make_async_copy(cols, hl.at[0], recv.at[8]).start()

    drain.append(lambda: pl.when(x == zh)(lambda: settle(st_in, send.at[13])))
    settle(hl.at[1], recv.at[4])
    settle(st_in, recv.at[9])
    st_sum[...] = st[...] + (st_in[0] + st_in[1] + st_in[2])
    lt = 0.9 * hl[1].reshape(256, 128) + 0.1 * st_sum[...]
    turned[...] = lt
    ur[0] = by_columns(lt, tile_of())

    def block_at(ref, d, *lead):
        r = pl.multiple_of((flip(c, d % 2) + 2 * flip(yl, d // 2 % 2)) * 32, 32)
        col = pl.multiple_of(flip(yh, d // 4) * 256, 256)
        return ref.at[(*lead, pl.ds(r, 32), pl.ds(col, 256))]

    for d in range(1, 8):
        remote(
            block_at(ur, d, 0), ur_in.at[0, d - 1], send.at[15], recv.at[10], y_peer(d)
        ).start()
    sent(ur_in.at[0], send.at[15])
    own = turned[pl.ds(pl.multiple_of(x * 64, 64), 64), :]
    la[ylc] = own
    for d in range(1, 4):
        remote(la.at[ylc], la.at[ylc], send.at[16], recv.at[11], y_peer(d)).start()
    sent(qg_in, send.at[16])
    lane = lax.broadcasted_iota(jnp.int32, (8, 128), 1)

    def sum_in_plane(n, values):
        v = jnp.zeros((8, 128), F32)
        for i, value in enumerate(values):
            v = jnp.where(lane == i, value, v)
        s_own[n] = v

        for d in range(1, 32):
            remote(s_own.at[n], s1_in.at[n, d - 1], s_sems.at[0, n], s_sems.at[1, n], plane_peer(d)).start()
        sent(s1_in.at[n], s_sems.at[0, n])

    def sum_along_z(n):
        settle(s1_in.at[n], s_sems.at[1, n])
        s1_sum[n] = s_own[n] + jnp.sum(s1_in[n], axis=0)

        for k in range(1, 16):
            remote(s1_sum.at[n], s2_in.at[n, k - 1], s_sems.at[2, n], s_sems.at[3, n], z_peer(k)).start()
        sent(s2_in.at[n], s_sems.at[2, n])

    def sums(n, count):
        settle(s2_in.at[n], s_sems.at[3, n])
        v = s1_sum[n] + jnp.sum(s2_in[n], axis=0)
        first = lax.broadcasted_iota(jnp.int32, (8, 128), 0) == 0
        picked = [jnp.where((lane == i) & first, v, 0.0) for i in range(count)]
        return [jnp.sum(jnp.sum(p, axis=1, keepdims=True), axis=0, keepdims=True) for p in picked]

    sum_in_plane(0, (total(own), total(piece[...])))
    settle(hl.at[0], recv.at[8])
    ur[1] = by_columns(hl[0].reshape(256, 128), tile_of())
    for d in range(1, 8):
        remote(
            block_at(ur, d, 1), ur_in.at[1, d - 1], send.at[0], recv.at[5], y_peer(d)
        ).start()
    drain.append(lambda: settle(ur_in.at[1], send.at[0]))

    settle(ur_in.at[0], recv.at[10])
    u_block = block_at(ur, 0, 0)[...]
    for d in range(7):
        u_block = u_block + ur_in[0, d]
    ub[...] = u_block
    block_at(uz, 0)[...] = u_block
    for d in range(1, 8):
        remote(ub, block_at(uz, 0), send.at[17], recv.at[12], y_peer(d)).start()
    sent(pr_in, send.at[17])
    sum_along_z(0)

    settle(uz.at[pl.ds(0, 112)], recv.at[12])
    rows_u = uz[...]
    su[...] = by_rows(tile_of(), rows_u)
    for k in range(1, 4):
        remote(su, su_in.at[k - 1], send.at[22], recv.at[17], x_peer(k)).start()
    sent(st_in, send.at[22])
    settle(ur_in.at[1], recv.at[5])
    r_block = block_at(ur, 0, 1)[...]
    for d in range(7):
        r_block = r_block + ur_in[1, d]
    right = 0.9 * rs_ref[...] + 0.1 * r_block
    right_ref[...] = right
    sum_in_plane(1, (total(right),))
    pl.when(z1 == yh)(lambda: settle(stat.at[:, 0], recv.at[3]))
    pl.when(z1 != yh)(lambda: settle(stat, recv.at[3]))
    qg[...] = by_rows((stat[...].reshape(256, 512),), rows_z).reshape(4, 64, 128)
    for k in range(1, 4):
        to = lax.rem(x + k, 4)
        remote(qg.at[to], qg_in.at[k - 1], send.at[12], recv.at[7], x_peer(k)).start()
    sent(qg_in, send.at[12])
    qu[...] = by_rows((stat[...].reshape(256, 512),), rows_u).reshape(4, 64, 128)
    for k in range(1, 4):
        to = lax.rem(x + k, 4)
        remote(qu.at[to], qu_in.at[k - 1], send.at[23], recv.at[18], x_peer(k)).start()
    sent(qg_in, send.at[23])
    sum_along_z(1)

    def assembled(slots):
        v = slots[...].reshape(4, 2, 32, 128)
        whole = jnp.concatenate([v[i, b] for b in range(2) for i in range(4)], axis=0)
        return whole.T

    settle(la.at[pl.ds(0, 3)], recv.at[11])
    lt_rows = assembled(la)
    uz_rows = pl.ds(pl.multiple_of(ylc * 32, 32), 32)
    pr[:, 0:256] = lt_rows
    left_ref[...] = pr[uz_rows, 0:256]

    settle(su_in, recv.at[17])
    s_u = su[...] + (su_in[0] + su_in[1] + su_in[2])
    settle(qg_in, recv.at[7])
    settle(qu_in, recv.at[18])
    left_total, grad_total = sums(0, 2)
    left_scale = jnp.sqrt(left_total / B + 1e-06)
    q_g = qg[x] + qg_in[0] + qg_in[1] + qg_in[2]
    q_u = qu[x] + qu_in[0] + qu_in[1] + qu_in[2]
    q_sum[...] = 0.9 * (5.0 * q_g - q_u / left_scale)
    qa[ylc] = q_sum[...]
    for d in range(1, 4):
        remote(q_sum, qa.at[ylc], send.at[24], recv.at[19], y_peer(d)).start()
    sent(qg_in, send.at[24])
    pr[...] = by_columns(0.1 * (5.0 * st_sum[...] - s_u / left_scale), tile_of())
    for d in range(1, 8):
        remote(block_at(pr, d), pr_in.at[d - 1], send.at[25], recv.at[20], y_peer(d)).start()
    sent(pr_in, send.at[25])
    pre_left = 5.0 * block_at(gz, 0)[...] - ub[...] / left_scale
    settle(qa.at[pl.ds(0, 3)], recv.at[19])
    turned[pl.ds(0, 128), :] = assembled(qa)[:, 0:128]
    turned[pl.ds(128, 128), :] = assembled(qa)[:, 128:256]
    low = turned[pl.ds(pl.multiple_of(ylc * 32, 32), 32), :]
    high = turned[pl.ds(pl.multiple_of(128 + ylc * 32, 32), 32), :]
    product = jnp.concatenate([low, high], axis=1) + block_at(pr, 0)[...]
    settle(pr_in, recv.at[20])
    for d in range(7):
        product = product + pr_in[d]
    (right_total,) = sums(1, 1)
    right_scale = jnp.sqrt(right_total / B + 1e-06)
    pre = 5.0 * pre_left - product / right_scale
    sum_in_plane(2, (total(pre),))
    sum_along_z(2)
    (pre_total,) = sums(2, 1)
    update_ref[...] = pre * (jnp.sqrt(grad_total + 1e-06) / jnp.sqrt(pre_total + 1e-06))

    for wait in drain:
        wait()


def local(activations, out_grads, left_stat, right_stat):
    vmem = pl.BlockSpec(memory_space=pltpu.VMEM)
    block = jax.ShapeDtypeStruct((32, 256), F32)
    bf16 = jnp.bfloat16
    shapes = [
        ((TOKENS, 256), bf16), ((TOKENS, 256), bf16),
        ((3, TOKENS, 256), bf16), ((TOKENS, 256), bf16),
        ((4, 2, 2, 2, 32, 512), F32), ((4, 2, 2, 32, 512), F32),
        ((4, 2, 2, 32, 512), F32), ((4, 2, 32, 512), F32),
        ((4, 2, 32, 512), F32), ((4, 3, 16, 512), F32),
        ((4, 16, 512), F32), ((4, 3, 16, 512), F32),
        ((4, 2, 32, 512), F32), ((2, 4, 64, 512), bf16), ((128, 512), F32),
        ((4, 2, 32, 512), bf16), ((32, 256), bf16),
        ((4, 2, 32, 128), F32), ((2, 4, 2, 32, 128), F32),
        ((256, 128), F32), ((3, 256, 128), F32), ((256, 128), F32),
        ((4, 64, 128), F32), ((3, 64, 128), F32),
        ((2, 128, 512), F32), ((2, 7, 32, 256), F32),
        ((4, 64, 128), F32), ((256, 128), F32), ((32, 256), F32), ((128, 512), F32),
        ((256, 128), F32), ((3, 256, 128), F32),
        ((4, 64, 128), F32), ((3, 64, 128), F32),
        ((128, 512), F32), ((7, 32, 256), F32),
        ((64, 128), F32), ((4, 64, 128), F32),
        ((3, 8, 128), F32), ((3, 31, 8, 128), F32),
        ((3, 8, 128), F32), ((3, 15, 8, 128), F32),
    ]
    dma = pltpu.SemaphoreType.DMA
    sems = [dma, dma((3, 2)), dma((26,)), dma((21,))] + [dma((4,))] * 12
    sems += [dma((4, 3)), pltpu.SemaphoreType.REGULAR((3,))]
    return pl.pallas_call(
        kernel,
        out_shape=(block, block, block),
        in_specs=[pl.BlockSpec(memory_space=pl.ANY)] * 2 + [vmem] * 2,
        out_specs=(vmem, vmem, vmem),
        scratch_shapes=[pltpu.VMEM(s, d) for s, d in shapes] + sems,
        compiler_params=pltpu.CompilerParams(
            collective_id=0, has_side_effects=True, vmem_limit_bytes=60 * 2**20
        ),
        cost_estimate=pl.CostEstimate(flops=2 * 10**9, bytes_accessed=4 * 10**6, transcendentals=0),
    )(activations, out_grads, left_stat, right_stat)


def solution(mesh):
    finer = Mesh(mesh.devices.reshape(16, 2, 2, 4, 2), ("z", "yl", "c", "x", "yh"))
    spec = P(DP, TENSOR)
    return jax.shard_map(
        local,
        mesh=finer,
        in_specs=(spec,) * 4,
        out_specs=(spec,) * 3,
        check_vma=False,
    )
```

time: 158 us -> 152 us (0.962)
  Pallas kernels: 154 us -> 148 us
    pallas_call x1, Pallas kernels: 154 us -> 148 us  [local(): pl.pallas_call(kernel, out_shape=(block, block, block), in_specs=[pl.Bloc...]
where the time goes in v2:
time: 152 us
  Pallas kernels  148 us (97%)
  local copies, waits for them, and re-layouts  2.77 us (2%)
    pallas_call x1, Pallas kernels, local(): pl.pallas_call(kernel, out_shape=(block, block, block), in_specs=[pl.Bloc...  148 us

profile of v2, /device:TPU:1, one launch (start us, length us, event | category | flops | bytes accessed | tf_op | source)
XLA Modules:
  0.0 151.8 jit_solution(17357132432029772643)
XLA Ops:
  0.6 148.4 %shard_map.67 = (f32[32,256]{1,0:T(8,128)}, f32[32,256]{1,0:T(8,128)}, f32[32,256]{1,0:T(8,128)}) custom-call(bf16[1536,256]{1,0:T(8,128)(2,1)} %a_ref.1, bf16[1536,256]{1,0:T(8,128)(2,1)} %o_ref.1, f32[32,256]{1,0:T(8,128)} %ls_ref.1, f32[32,256]{1,0:T(8,128)} %rs_ref.1), custom_call_target="tpu_custom_call" | custom-call | flops 2000000000 | bytes 4000000 | tf_op jit(solution)/shard_map/pallas_call | solution.py:525
  149.0 0.0 copy-start.1
  149.0 1.4 copy.10
  150.4 0.0 copy-done.1
  150.4 0.0 copy-start
  150.4 0.6 copy.11
  151.0 0.2 copy-done
  151.2 0.6 copy.12
Async XLA Ops:
  149.0 1.4 copy-start.1
  150.4 0.8 copy-start

commit v3 on v2

--- a/solution.py
+++ b/solution.py
@@ -29,12 +29,13 @@
 
 
 def by_rows(a, b):
-    high, low = parts(b)
     over = ((1,), (1,))
-    small = dot(a[0], low, over)
-    if len(a) == 2:
-        small = small + dot(a[1], high, over)
-    return dot(a[0], high, over) + small
+    product = dot(a[0], b[0], over)
+    for low in a[1:]:
+        product = product + dot(low, b[0], over)
+    for low in b[1:]:
+        product = product + dot(a[0], low, over)
+    return product
 
 
 def by_columns(a, b):
@@ -48,9 +49,9 @@
 
 
 def kernel(
-    a_ref, o_ref, ls_ref, rs_ref, left_ref, right_ref, update_ref,
+    a_ref, o_ref, ls_ref, rs_ref, out_ref,
     a_own, o_own, a_in, o_in, part, c_in, c_sum, y_in, tile, z1_in, z1_sum, z2_in, grad, g_parts, gz, stat, rs_half,
-    ls_in, hl, st, st_in, st_sum, qg, qg_in, ur, ur_in, la, turned, ub, uz, su, su_in, qu, qu_in,
+    ls_in, hl, st, st_in, st_sum, qg, qg_in, ur, ur_in, la, turned, ub, u_half, uz, su, su_in, qu, qu_in,
     pr, pr_in, q_sum, qa, s_own, s1_in, s1_sum, s2_in,
     a_send, a_recv, send, recv, c_send, c_recv, y_send, y_recv, z_send, z_recv, z2_send, z2_recv,
     far_send, far_recv, near_send, near_recv, s_sems, relay,
@@ -319,18 +320,34 @@
     home = 4 * zh + 2 * yh + zb
     gz_rows = gz.at[pl.ds(pl.multiple_of(ylc * 32 + flip(z1, yh) * 16, 16), 16)]
     piece = grad.at[zh, zb, mine]
-    for d in range(1, 8):
-        remote(piece, gz_rows, send.at[9], recv.at[6], y_peer(d, z=home)).start()
-    gz_send = remote(piece, gz_rows, send.at[10], recv.at[6], at(z=home))
-    pl.when(home == z)(lambda: pltpu.make_async_copy(piece, gz_rows, recv.at[6]).start())
-    pl.when(home != z)(lambda: gz_send.start())
-    sent(gz.at[pl.ds(0, 112)], send.at[9])
+    gz_other = gz.at[pl.ds(pl.multiple_of(ylc * 32 + 16, 16), 16)]
+    gz_send = remote(piece, gz_rows, send.at[10], recv.at[21], at(z=home))
+
+    @pl.when(home == z)
+    def _():
+        for d in range(1, 8):
+            remote(piece, gz_rows, send.at[9], recv.at[6], y_peer(d)).start()
+        pltpu.make_async_copy(piece, gz_rows, recv.at[6]).start()
+
+    @pl.when(home != z)
+    def _():
+        gz_send.start()
+
+    @pl.when(home == z)
+    def _():
+        settle(gz_other, recv.at[21])
+        for d in range(1, 8):
+            remote(gz_other, gz_other, send.at[18], recv.at[6], y_peer(d)).start()
+
     drain.append(lambda: pl.when(home != z)(gz_send.wait_send))
+    drain.append(lambda: pl.when(home == z)(lambda: settle(gz.at[pl.ds(0, 112)], send.at[9])))
+    drain.append(lambda: pl.when(home == z)(lambda: settle(gz.at[pl.ds(0, 112)], send.at[18])))
     z3_end(1)
     z3_end(2)
     z3_end(3)
-    settle(gz, recv.at[6])
-    rows_z = gz[...]
+    pl.when(home == z)(lambda: settle(gz.at[pl.ds(0, 112)], recv.at[6]))
+    pl.when(home != z)(lambda: settle(gz, recv.at[6]))
+    rows_z = parts(gz[...])
 
     def tile_of():
         return g_parts[0].reshape(256, 512), g_parts[1].reshape(256, 512)
@@ -370,10 +387,10 @@
     for d in range(1, 4):
         remote(la.at[ylc], la.at[ylc], send.at[16], recv.at[11], y_peer(d)).start()
     sent(qg_in, send.at[16])
-    lane = lax.broadcasted_iota(jnp.int32, (8, 128), 1)
+    lane = lax.broadcasted_iota(jnp.int32, (1, 128), 1)
 
     def sum_in_plane(n, values):
-        v = jnp.zeros((8, 128), F32)
+        v = jnp.zeros((1, 128), F32)
         for i, value in enumerate(values):
             v = jnp.where(lane == i, value, v)
         s_own[n] = v
@@ -393,11 +410,9 @@
     def sums(n, count):
         settle(s2_in.at[n], s_sems.at[3, n])
         v = s1_sum[n] + jnp.sum(s2_in[n], axis=0)
-        first = lax.broadcasted_iota(jnp.int32, (8, 128), 0) == 0
-        picked = [jnp.where((lane == i) & first, v, 0.0) for i in range(count)]
-        return [jnp.sum(jnp.sum(p, axis=1, keepdims=True), axis=0, keepdims=True) for p in picked]
-
-    sum_in_plane(0, (total(own), total(piece[...])))
+        picked = [jnp.where(lane == i, v, 0.0) for i in range(count)]
+        return [jnp.sum(p, axis=1, keepdims=True) for p in picked]
+
     settle(hl.at[0], recv.at[8])
     ur[1] = by_columns(hl[0].reshape(256, 128), tile_of())
     for d in range(1, 8):
@@ -405,30 +420,32 @@
             block_at(ur, d, 1), ur_in.at[1, d - 1], send.at[0], recv.at[5], y_peer(d)
         ).start()
     drain.append(lambda: settle(ur_in.at[1], send.at[0]))
+    sum_in_plane(0, (total(own), total(piece[...])))
 
     settle(ur_in.at[0], recv.at[10])
     u_block = block_at(ur, 0, 0)[...]
     for d in range(7):
         u_block = u_block + ur_in[0, d]
     ub[...] = u_block
-    block_at(uz, 0)[...] = u_block
+    u_half[...] = u_block.astype(jnp.bfloat16)
+    block_at(uz, 0)[...] = u_half[...]
     for d in range(1, 8):
-        remote(ub, block_at(uz, 0), send.at[17], recv.at[12], y_peer(d)).start()
-    sent(pr_in, send.at[17])
+        remote(u_half, block_at(uz, 0), send.at[17], recv.at[12], y_peer(d)).start()
+    sent(uz.at[pl.ds(0, 112)], send.at[17])
     sum_along_z(0)
 
     settle(uz.at[pl.ds(0, 112)], recv.at[12])
-    rows_u = uz[...]
-    su[...] = by_rows(tile_of(), rows_u)
+    rows_u = (uz[...],)
+    su[...] = by_rows(tile_of(), rows_u).astype(jnp.bfloat16)
     for k in range(1, 4):
         remote(su, su_in.at[k - 1], send.at[22], recv.at[17], x_peer(k)).start()
-    sent(st_in, send.at[22])
+    sent(su_in, send.at[22])
     settle(ur_in.at[1], recv.at[5])
     r_block = block_at(ur, 0, 1)[...]
     for d in range(7):
         r_block = r_block + ur_in[1, d]
     right = 0.9 * rs_ref[...] + 0.1 * r_block
-    right_ref[...] = right
+    out_ref[1] = right
     sum_in_plane(1, (total(right),))
     pl.when(z1 == yh)(lambda: settle(stat.at[:, 0], recv.at[3]))
     pl.when(z1 != yh)(lambda: settle(stat, recv.at[3]))
@@ -437,11 +454,11 @@
         to = lax.rem(x + k, 4)
         remote(qg.at[to], qg_in.at[k - 1], send.at[12], recv.at[7], x_peer(k)).start()
     sent(qg_in, send.at[12])
-    qu[...] = by_rows((stat[...].reshape(256, 512),), rows_u).reshape(4, 64, 128)
+    qu[...] = by_rows((stat[...].reshape(256, 512),), rows_u).astype(jnp.bfloat16).reshape(4, 64, 128)
     for k in range(1, 4):
         to = lax.rem(x + k, 4)
         remote(qu.at[to], qu_in.at[k - 1], send.at[23], recv.at[18], x_peer(k)).start()
-    sent(qg_in, send.at[23])
+    sent(qu_in, send.at[23])
     sum_along_z(1)
 
     def assembled(slots):
@@ -453,16 +470,20 @@
     lt_rows = assembled(la)
     uz_rows = pl.ds(pl.multiple_of(ylc * 32, 32), 32)
     pr[:, 0:256] = lt_rows
-    left_ref[...] = pr[uz_rows, 0:256]
+    out_ref[0] = pr[uz_rows, 0:256]
 
     settle(su_in, recv.at[17])
-    s_u = su[...] + (su_in[0] + su_in[1] + su_in[2])
+    s_u = su[...].astype(F32)
+    for i in range(3):
+        s_u = s_u + su_in[i].astype(F32)
     settle(qg_in, recv.at[7])
     settle(qu_in, recv.at[18])
     left_total, grad_total = sums(0, 2)
     left_scale = jnp.sqrt(left_total / B + 1e-06)
     q_g = qg[x] + qg_in[0] + qg_in[1] + qg_in[2]
-    q_u = qu[x] + qu_in[0] + qu_in[1] + qu_in[2]
+    q_u = qu[x].astype(F32)
+    for i in range(3):
+        q_u = q_u + qu_in[i].astype(F32)
     q_sum[...] = 0.9 * (5.0 * q_g - q_u / left_scale)
     qa[ylc] = q_sum[...]
     for d in range(1, 4):
@@ -488,7 +509,7 @@
     sum_in_plane(2, (total(pre),))
     sum_along_z(2)
     (pre_total,) = sums(2, 1)
-    update_ref[...] = pre * (jnp.sqrt(grad_total + 1e-06) / jnp.sqrt(pre_total + 1e-06))
+    out_ref[2] = pre * (jnp.sqrt(grad_total + 1e-06) / jnp.sqrt(pre_total + 1e-06))
 
     for wait in drain:
         wait()
@@ -511,28 +532,29 @@
         ((256, 128), F32), ((3, 256, 128), F32), ((256, 128), F32),
         ((4, 64, 128), F32), ((3, 64, 128), F32),
         ((2, 128, 512), F32), ((2, 7, 32, 256), F32),
-        ((4, 64, 128), F32), ((256, 128), F32), ((32, 256), F32), ((128, 512), F32),
-        ((256, 128), F32), ((3, 256, 128), F32),
-        ((4, 64, 128), F32), ((3, 64, 128), F32),
+        ((4, 64, 128), F32), ((256, 128), F32), ((32, 256), F32), ((32, 256), bf16), ((128, 512), bf16),
+        ((256, 128), bf16), ((3, 256, 128), bf16),
+        ((4, 64, 128), bf16), ((3, 64, 128), bf16),
         ((128, 512), F32), ((7, 32, 256), F32),
         ((64, 128), F32), ((4, 64, 128), F32),
-        ((3, 8, 128), F32), ((3, 31, 8, 128), F32),
-        ((3, 8, 128), F32), ((3, 15, 8, 128), F32),
+        ((3, 1, 128), F32), ((3, 31, 1, 128), F32),
+        ((3, 1, 128), F32), ((3, 15, 1, 128), F32),
     ]
     dma = pltpu.SemaphoreType.DMA
-    sems = [dma, dma((3, 2)), dma((26,)), dma((21,))] + [dma((4,))] * 12
+    sems = [dma, dma((3, 2)), dma((26,)), dma((22,))] + [dma((4,))] * 12
     sems += [dma((4, 3)), pltpu.SemaphoreType.REGULAR((3,))]
-    return pl.pallas_call(
+    out = pl.pallas_call(
         kernel,
-        out_shape=(block, block, block),
+        out_shape=jax.ShapeDtypeStruct((3, 32, 256), F32),
         in_specs=[pl.BlockSpec(memory_space=pl.ANY)] * 2 + [vmem] * 2,
-        out_specs=(vmem, vmem, vmem),
+        out_specs=vmem,
         scratch_shapes=[pltpu.VMEM(s, d) for s, d in shapes] + sems,
         compiler_params=pltpu.CompilerParams(
             collective_id=0, has_side_effects=True, vmem_limit_bytes=60 * 2**20
         ),
         cost_estimate=pl.CostEstimate(flops=2 * 10**9, bytes_accessed=4 * 10**6, transcendentals=0),
     )(activations, out_grads, left_stat, right_stat)
+    return out[0], out[1], out[2]
 
 
 def solution(mesh):

time: 152 us -> 141 us (0.928)
  Pallas kernels: 148 us -> 138 us
    pallas_call x1, Pallas kernels: 148 us -> 138 us  [local(): pl.pallas_call(kernel, out_shape=jax.ShapeDtypeStruct((3, 32, 256), F32),...]
    unnamed x7 -> x0, local copies, waits for them, and re-layouts: 2.77 us -> none
where the time goes in v3:
time: 141 us; the launch traced here: 140 us
  Pallas kernels  138 us (98%)
  local copies, waits for them, and re-layouts  1.43 us (1%)
    pallas_call x1, Pallas kernels, local(): pl.pallas_call(kernel, out_shape=jax.ShapeDtypeStruct((3, 32, 256), F32),...  138 us

profile of v3, /device:TPU:1, one launch (start us, length us, event | category | flops | bytes accessed | tf_op | source)
XLA Modules:
  0.0 140.3 jit_solution(11420383284771560540)
XLA Ops:
  0.6 138.2 %shard_map.67 = f32[3,32,256]{2,1,0:T(8,128)} custom-call(bf16[1536,256]{1,0:T(8,128)(2,1)} %a_ref.1, bf16[1536,256]{1,0:T(8,128)(2,1)} %o_ref.1, f32[32,256]{1,0:T(8,128)} %ls_ref.1, f32[32,256]{1,0:T(8,128)} %rs_ref.1), custom_call_target="tpu_custom_call" | custom-call | flops 2000000000 | bytes 4000000 | tf_op jit(solution)/shard_map/pallas_call | solution.py:546
  138.8 1.4 %slice_bitcast_fusion = (f32[32,256]{1,0:T(8,128)}, f32[32,256]{1,0:T(8,128)}, f32[32,256]{1,0:T(8,128)}) fusion(f32[3,32,256]{2,1,0:T(8,128)} %shard_map.67), kind=kLoop, calls=%fused_computation | loop fusion | bytes 196608 | tf_op jit(solution)/shard_map/squeeze | solution.py:557

commit v4 on v3

--- a/solution.py
+++ b/solution.py
@@ -10,8 +10,12 @@
 TENSOR = ("x", "yh")
 MESH = pl.DeviceIdType.MESH
 F32 = jnp.float32
-NEAR = (1, 15, 2)
-FAR = (4, 12, 8)
+NEAR = (2, 1, 15)
+FAR = (8, 4, 12)
+ALONG_X = (2, 1, 3)
+ALONG_Y = (4, 5, 6, 7, 2, 3, 1)
+ALONG_Z = (8, 7, 9, 6, 10, 5, 11, 4, 12, 3, 13, 2, 14, 1, 15)
+IN_PLANE = sorted(range(1, 32), key=lambda d: -((0, 1, 2, 1)[d // 2 % 4] + (0, 2, 1, 1)[d % 2 + d // 16 * 2]))
 DIRECT = (3,)
 BLOCKS = (0, 3, 1, 2)
 TOKENS = 1536
@@ -293,7 +297,7 @@
     @pl.when(x == zh)
     def _():
         settle(ls_in, recv.at[2])
-        for k in range(1, 4):
+        for k in ALONG_X:
             remote(ls_in, hl.at[1], send.at[6], recv.at[4], x_peer(k)).start()
         pltpu.make_async_copy(ls_in, hl.at[1], recv.at[4]).start()
 
@@ -325,7 +329,7 @@
 
     @pl.when(home == z)
     def _():
-        for d in range(1, 8):
+        for d in ALONG_Y:
             remote(piece, gz_rows, send.at[9], recv.at[6], y_peer(d)).start()
         pltpu.make_async_copy(piece, gz_rows, recv.at[6]).start()
 
@@ -336,7 +340,7 @@
     @pl.when(home == z)
     def _():
         settle(gz_other, recv.at[21])
-        for d in range(1, 8):
+        for d in ALONG_Y:
             remote(gz_other, gz_other, send.at[18], recv.at[6], y_peer(d)).start()
 
     drain.append(lambda: pl.when(home != z)(gz_send.wait_send))
@@ -353,14 +357,14 @@
         return g_parts[0].reshape(256, 512), g_parts[1].reshape(256, 512)
 
     st[...] = by_rows(tile_of(), rows_z)
-    for k in range(1, 4):
+    for k in ALONG_X:
         remote(st, st_in.at[k - 1], send.at[14], recv.at[9], x_peer(k)).start()
     sent(st_in, send.at[14])
 
     @pl.when(x == zh)
     def _():
         cols = grad.at[:, :, :, pl.ds(pl.multiple_of(z % 4 * 128, 128), 128)]
-        for k in range(1, 4):
+        for k in ALONG_X:
             remote(cols, hl.at[0], send.at[13], recv.at[8], x_peer(k)).start()
         pltpu.make_async_copy(cols, hl.at[0], recv.at[8]).start()
 
@@ -377,7 +381,7 @@
         col = pl.multiple_of(flip(yh, d // 4) * 256, 256)
         return ref.at[(*lead, pl.ds(r, 32), pl.ds(col, 256))]
 
-    for d in range(1, 8):
+    for d in ALONG_Y:
         remote(
             block_at(ur, d, 0), ur_in.at[0, d - 1], send.at[15], recv.at[10], y_peer(d)
         ).start()
@@ -395,7 +399,7 @@
             v = jnp.where(lane == i, value, v)
         s_own[n] = v
 
-        for d in range(1, 32):
+        for d in IN_PLANE:
             remote(s_own.at[n], s1_in.at[n, d - 1], s_sems.at[0, n], s_sems.at[1, n], plane_peer(d)).start()
         sent(s1_in.at[n], s_sems.at[0, n])
 
@@ -403,7 +407,7 @@
         settle(s1_in.at[n], s_sems.at[1, n])
         s1_sum[n] = s_own[n] + jnp.sum(s1_in[n], axis=0)
 
-        for k in range(1, 16):
+        for k in ALONG_Z:
             remote(s1_sum.at[n], s2_in.at[n, k - 1], s_sems.at[2, n], s_sems.at[3, n], z_peer(k)).start()
         sent(s2_in.at[n], s_sems.at[2, n])
 
@@ -415,7 +419,7 @@
 
     settle(hl.at[0], recv.at[8])
     ur[1] = by_columns(hl[0].reshape(256, 128), tile_of())
-    for d in range(1, 8):
+    for d in ALONG_Y:
         remote(
             block_at(ur, d, 1), ur_in.at[1, d - 1], send.at[0], recv.at[5], y_peer(d)
         ).start()
@@ -429,7 +433,7 @@
     ub[...] = u_block
     u_half[...] = u_block.astype(jnp.bfloat16)
     block_at(uz, 0)[...] = u_half[...]
-    for d in range(1, 8):
+    for d in ALONG_Y:
         remote(u_half, block_at(uz, 0), send.at[17], recv.at[12], y_peer(d)).start()
     sent(uz.at[pl.ds(0, 112)], send.at[17])
     sum_along_z(0)
@@ -437,7 +441,7 @@
     settle(uz.at[pl.ds(0, 112)], recv.at[12])
     rows_u = (uz[...],)
     su[...] = by_rows(tile_of(), rows_u).astype(jnp.bfloat16)
-    for k in range(1, 4):
+    for k in ALONG_X:
         remote(su, su_in.at[k - 1], send.at[22], recv.at[17], x_peer(k)).start()
     sent(su_in, send.at[22])
     settle(ur_in.at[1], recv.at[5])
@@ -450,12 +454,12 @@
     pl.when(z1 == yh)(lambda: settle(stat.at[:, 0], recv.at[3]))
     pl.when(z1 != yh)(lambda: settle(stat, recv.at[3]))
     qg[...] = by_rows((stat[...].reshape(256, 512),), rows_z).reshape(4, 64, 128)
-    for k in range(1, 4):
+    for k in ALONG_X:
         to = lax.rem(x + k, 4)
         remote(qg.at[to], qg_in.at[k - 1], send.at[12], recv.at[7], x_peer(k)).start()
     sent(qg_in, send.at[12])
     qu[...] = by_rows((stat[...].reshape(256, 512),), rows_u).astype(jnp.bfloat16).reshape(4, 64, 128)
-    for k in range(1, 4):
+    for k in ALONG_X:
         to = lax.rem(x + k, 4)
         remote(qu.at[to], qu_in.at[k - 1], send.at[23], recv.at[18], x_peer(k)).start()
     sent(qu_in, send.at[23])
@@ -490,7 +494,7 @@
         remote(q_sum, qa.at[ylc], send.at[24], recv.at[19], y_peer(d)).start()
     sent(qg_in, send.at[24])
     pr[...] = by_columns(0.1 * (5.0 * st_sum[...] - s_u / left_scale), tile_of())
-    for d in range(1, 8):
+    for d in ALONG_Y:
         remote(block_at(pr, d), pr_in.at[d - 1], send.at[25], recv.at[20], y_peer(d)).start()
     sent(pr_in, send.at[25])
     pre_left = 5.0 * block_at(gz, 0)[...] - ub[...] / left_scale

time: 141 us -> 136 us (0.965)
  Pallas kernels: 138 us -> 134 us
    pallas_call x1, Pallas kernels: 138 us -> 134 us  [local(): pl.pallas_call(kernel, out_shape=jax.ShapeDtypeStruct((3, 32, 256), F32),...]
where the time goes in v4:
time: 136 us
  Pallas kernels  134 us (99%)
  local copies, waits for them, and re-layouts  1.43 us (1%)
    pallas_call x1, Pallas kernels, local(): pl.pallas_call(kernel, out_shape=jax.ShapeDtypeStruct((3, 32, 256), F32),...  134 us

profile of v4, /device:TPU:1, one launch (start us, length us, event | category | flops | bytes accessed | tf_op | source)
XLA Modules:
  0.0 135.7 jit_solution(4893880082535733370)
XLA Ops:
  0.6 133.6 %shard_map.67 = f32[3,32,256]{2,1,0:T(8,128)} custom-call(bf16[1536,256]{1,0:T(8,128)(2,1)} %a_ref.1, bf16[1536,256]{1,0:T(8,128)(2,1)} %o_ref.1, f32[32,256]{1,0:T(8,128)} %ls_ref.1, f32[32,256]{1,0:T(8,128)} %rs_ref.1), custom_call_target="tpu_custom_call" | custom-call | flops 2000000000 | bytes 4000000 | tf_op jit(solution)/shard_map/pallas_call | solution.py:550
  134.3 1.4 %slice_bitcast_fusion = (f32[32,256]{1,0:T(8,128)}, f32[32,256]{1,0:T(8,128)}, f32[32,256]{1,0:T(8,128)}) fusion(f32[3,32,256]{2,1,0:T(8,128)} %shard_map.67), kind=kLoop, calls=%fused_computation | loop fusion | bytes 196608 | tf_op jit(solution)/shard_map/squeeze | solution.py:561

commit v5 on v4

--- a/solution.py
+++ b/solution.py
@@ -53,8 +53,8 @@
 
 
 def kernel(
-    a_ref, o_ref, ls_ref, rs_ref, out_ref,
-    a_own, o_own, a_in, o_in, part, c_in, c_sum, y_in, tile, z1_in, z1_sum, z2_in, grad, g_parts, gz, stat, rs_half,
+    a_ref, o_ref, ls_hbm, rs_hbm, out_ref,
+    a_own, o_own, ls_ref, rs_ref, a_in, o_in, part, c_in, c_sum, y_in, tile, z1_in, z1_sum, z2_in, grad, g_parts, gz, stat, rs_half,
     ls_in, hl, st, st_in, st_sum, qg, qg_in, ur, ur_in, la, turned, ub, u_half, uz, su, su_in, qu, qu_in,
     pr, pr_in, q_sum, qa, s_own, s1_in, s1_sum, s2_in,
     a_send, a_recv, send, recv, c_send, c_recv, y_send, y_recv, z_send, z_recv, z2_send, z2_recv,
@@ -108,6 +108,8 @@
     copies = [
         pltpu.make_async_copy(a_ref, a_own, send.at[7]),
         pltpu.make_async_copy(o_ref, o_own, send.at[8]),
+        pltpu.make_async_copy(ls_hbm, ls_ref, send.at[20]),
+        pltpu.make_async_copy(rs_hbm, rs_ref, send.at[21]),
     ]
     for copy in copies:
         copy.start()
@@ -225,9 +227,9 @@
         g_parts[0, xb] = high
         g_parts[1, xb] = low
 
-    rs_half[...] = rs_ref[...].astype(jnp.bfloat16)
     for copy in copies:
         copy.wait()
+    rs_half[...] = rs_ref[...].astype(jnp.bfloat16)
     terms(0, True)
     pl.semaphore_wait(relay.at[0], 4)
     for k in (3, 4, 12, 13):
@@ -525,6 +527,7 @@
     bf16 = jnp.bfloat16
     shapes = [
         ((TOKENS, 256), bf16), ((TOKENS, 256), bf16),
+        ((32, 256), F32), ((32, 256), F32),
         ((3, TOKENS, 256), bf16), ((TOKENS, 256), bf16),
         ((4, 2, 2, 2, 32, 512), F32), ((4, 2, 2, 32, 512), F32),
         ((4, 2, 2, 32, 512), F32), ((4, 2, 32, 512), F32),
@@ -550,7 +553,7 @@
     out = pl.pallas_call(
         kernel,
         out_shape=jax.ShapeDtypeStruct((3, 32, 256), F32),
-        in_specs=[pl.BlockSpec(memory_space=pl.ANY)] * 2 + [vmem] * 2,
+        in_specs=[pl.BlockSpec(memory_space=pl.ANY)] * 4,
         out_specs=vmem,
         scratch_shapes=[pltpu.VMEM(s, d) for s, d in shapes] + sems,
         compiler_params=pltpu.CompilerParams(

time: 136 us -> 137 us (level)
  no operation moved by 1% of the time
where the time goes in v5:
time: 137 us; the launch traced here: 136 us
  Pallas kernels  134 us (98%)
  local copies, waits for them, and re-layouts  1.43 us (1%)
    pallas_call x1, Pallas kernels, local(): pl.pallas_call(kernel, out_shape=jax.ShapeDtypeStruct((3, 32, 256), F32),...  134 us

profile of v5, /device:TPU:1, one launch (start us, length us, event | category | flops | bytes accessed | tf_op | source)
XLA Modules:
  0.0 136.5 jit_solution(15058710401528304090)
XLA Ops:
  0.6 134.4 %shard_map.67 = f32[3,32,256]{2,1,0:T(8,128)} custom-call(bf16[1536,256]{1,0:T(8,128)(2,1)} %a_ref.1, bf16[1536,256]{1,0:T(8,128)(2,1)} %o_ref.1, f32[32,256]{1,0:T(8,128)} %ls_hbm.1, f32[32,256]{1,0:T(8,128)} %rs_hbm.1), custom_call_target="tpu_custom_call" | custom-call | flops 2000000000 | bytes 4000000 | tf_op jit(solution)/shard_map/pallas_call | solution.py:553
  135.0 1.4 %slice_bitcast_fusion = (f32[32,256]{1,0:T(8,128)}, f32[32,256]{1,0:T(8,128)}, f32[32,256]{1,0:T(8,128)}) fusion(f32[3,32,256]{2,1,0:T(8,128)} %shard_map.67), kind=kLoop, calls=%fused_computation | loop fusion | bytes 196608 | tf_op jit(solution)/shard_map/squeeze | solution.py:564
